TPU v7x, 512 devices: a whole 4x4x16 slice. The times are simulated.
512 devices in a mesh: section: 128 (over z, y, core), dp: 4 (over x).
Axes of the slice: x: 4, y: 4, z: 16, core: 2. Of those that a mesh axis runs over, the one named last changes fastest.
Arguments:
- features: bfloat16 [4, 32768, 128], P('dp', 'section'), may hold values from -6 to 6
- grad_out: bfloat16 [4, 32768, 512], P('dp', 'section'), may hold values from -0.015625 to 0.015625
- w_first: bfloat16 [128, 512], replicated, may hold values from -0.5 to 0.5
- w_second: bfloat16 [512, 512], replicated, may hold values from -0.25 to 0.25
- tile_values: bfloat16 [4, 1024, 128, 128], P('dp', 'section'), may hold values from -0.25 to 0.25
- tile_rows: int32 [4, 1024], P('dp', 'section'), may hold values from 0 to 1, as said below
- tile_cols: int32 [4, 1024], P('dp', 'section'), may hold values from 0 to 5, as said below
- tile_count: int32 [4, 128], P('dp', 'section'), may hold values from 2 to 8, as said below
Outputs:
- grad_w1_t: float32 [512, 128], P(('section', 'dp'))
- grad_w2: float32 [512, 512], P(('section', 'dp'))
Inputs may be any that keep to these rules, and one draw needn't show every extreme that they name: Within one device, the pairs (tile_rows, tile_cols) of its slots are all different. `tile_cols`: blocks 0 to 1 are the previous device's, 2 to 3 the own, the rest the next device's. `tile_count`: in every graph batch some device uses all 8 slots; slots at or above a device's count hold no tile.
All inputs are finite; a program needn't handle non-finite values.
Results may differ from a plain program's by a relative error of at most 0.013.
Values may be sent and summed in bfloat16 or wider, within the bound.
No kernel may reach another device: no remote copies, remote signals or barrier semaphores. Data moves between devices by JAX's collectives and lax.ppermute only.
A program may use at most 64 MiB of HBM per device.

v0:
```python
import jax
import jax.numpy as jnp
from jax import lax
from jax.sharding import PartitionSpec as P


def with_halo(block, sides, width):
    for axis, dim in sides:
        count = lax.axis_size(axis)
        forward = [(i, i + 1) for i in range(count - 1)]
        backward = [(target, source) for source, target in forward]
        low = lax.ppermute(
            lax.slice_in_dim(block, block.shape[dim] - width, None, axis=dim), axis, forward
        )
        high = lax.ppermute(lax.slice_in_dim(block, 0, width, axis=dim), axis, backward)
        block = jnp.concatenate([low, block, high], axis=dim)
    return block


def shifted(block, axis, distance):
    devices = range(lax.axis_size(axis))
    route = [(i - distance, i) for i in devices if i - distance in devices]
    return lax.ppermute(block, axis, route)


def gelu_pair(inputs_in):
    values, pullback = jax.vjp(lambda entry: jax.nn.gelu(entry, approximate=True), inputs_in)
    slopes = pullback(jnp.ones_like(inputs_in))[0]
    return (values, slopes)


def tile_sums(blocks, tile_vals, row_ids, col_ids, live_count, row_blocks):
    columns = blocks.shape[2]
    tile_size = blocks.shape[1]
    group_count = (live_count + 7) // 8

    def tile_advance(group, total):
        first = group * 8
        live_slot = first + jnp.arange(8, dtype=jnp.int32) < live_count
        picked = jnp.take(blocks, col_ids, axis=0)
        product = jnp.einsum("tab,tbw->taw", tile_vals, picked, preferred_element_type=jnp.float32)
        onehot = (
            (row_ids[None, :] == jnp.arange(row_blocks, dtype=jnp.int32)[:, None])
            & live_slot[None, :]
        ).astype(jnp.float32)
        return total + jnp.einsum("rt,taw->raw", onehot, product, precision=lax.Precision.HIGHEST)

    start_total = jnp.zeros((row_blocks, tile_size, columns), jnp.float32)
    return lax.fori_loop(0, group_count, tile_advance, start_total)


def spread_sums(own_blocks, tile_vals, row_ids, col_ids, live_count, row_blocks):
    columns = own_blocks.shape[2]
    tile_size = own_blocks.shape[1]
    group_count = (live_count + 7) // 8

    def spread_advance(group, total):
        first = group * 8
        live_slot = first + jnp.arange(8, dtype=jnp.int32) < live_count
        picked = jnp.take(own_blocks, row_ids, axis=0)
        product = jnp.einsum("tab,taw->tbw", tile_vals, picked, preferred_element_type=jnp.float32)
        onehot = (
            (col_ids[None, :] == jnp.arange(3 * row_blocks, dtype=jnp.int32)[:, None])
            & live_slot[None, :]
        ).astype(jnp.float32)
        return total + jnp.einsum("ct,tbw->cbw", onehot, product, precision=lax.Precision.HIGHEST)

    start_total = jnp.zeros((3 * row_blocks, tile_size, columns), jnp.float32)
    return lax.fori_loop(0, group_count, spread_advance, start_total)


def body(features, grad_out, w_first, w_second, tile_values, tile_rows, tile_cols, tile_count):
    inputs_here = features[0]
    cotangent = grad_out[0]
    tile_vals = tile_values[0]
    row_ids = tile_rows[0]
    col_ids = tile_cols[0]
    live_count = tile_count[0, 0]
    node_dev = inputs_here.shape[0]
    tile_size = tile_vals.shape[1]
    row_blocks = node_dev // tile_size
    hidden_units = w_second.shape[0]
    in_features = w_first.shape[0]
    feature_window = with_halo(inputs_here, (("section", 0),), node_dev)
    agg1 = tile_sums(
        feature_window.reshape(3 * row_blocks, tile_size, in_features),
        tile_vals,
        row_ids,
        col_ids,
        live_count,
        row_blocks,
    )
    agg1 = agg1.reshape(node_dev, in_features).astype(jnp.bfloat16)
    pre1 = jnp.dot(agg1, w_first, preferred_element_type=jnp.float32)
    hid1, slope1 = gelu_pair(pre1)
    hid1 = hid1.astype(jnp.bfloat16)
    hidden_window = with_halo(hid1, (("section", 0),), node_dev)
    agg2 = tile_sums(
        hidden_window.reshape(3 * row_blocks, tile_size, hidden_units),
        tile_vals,
        row_ids,
        col_ids,
        live_count,
        row_blocks,
    )
    agg2 = agg2.reshape(node_dev, hidden_units).astype(jnp.bfloat16)
    pre2 = jnp.dot(agg2, w_second, preferred_element_type=jnp.float32)
    unused, slope2 = gelu_pair(pre2)
    dpre2 = (cotangent.astype(jnp.float32) * slope2).astype(jnp.bfloat16)
    dagg2 = lax.dot_general(
        dpre2, w_second, (((1,), (1,)), ((), ())), preferred_element_type=jnp.float32
    ).astype(jnp.bfloat16)
    own_blocks = dagg2.reshape(row_blocks, tile_size, hidden_units)
    spread = spread_sums(own_blocks, tile_vals, row_ids, col_ids, live_count, row_blocks)
    from_after = shifted(spread[:row_blocks].astype(jnp.bfloat16), "section", -1).astype(
        jnp.float32
    )
    from_before = shifted(spread[2 * row_blocks :].astype(jnp.bfloat16), "section", 1).astype(
        jnp.float32
    )
    dhid1 = spread[row_blocks : 2 * row_blocks] + from_after + from_before
    dhid1 = dhid1.reshape(node_dev, hidden_units)
    dpre1 = (dhid1 * slope1).astype(jnp.bfloat16)
    first_part = lax.dot_general(
        dpre1, agg1, (((0,), (0,)), ((), ())), preferred_element_type=jnp.float32
    )
    second_part = lax.dot_general(
        agg2, dpre2, (((0,), (0,)), ((), ())), preferred_element_type=jnp.float32
    )
    gradients = lax.psum_scatter(
        jnp.concatenate([first_part, second_part], axis=1),
        ("section", "dp"),
        scatter_dimension=0,
        tiled=True,
    )
    return (gradients[:, :in_features], gradients[:, in_features:])


def solution(mesh):
    placed = (
        P("dp", "section", None),
        P("dp", "section", None),
        P(),
        P(),
        P("dp", "section", None, None),
        P("dp", "section"),
        P("dp", "section"),
        P("dp", "section"),
    )
    return jax.shard_map(
        body,
        mesh=mesh,
        in_specs=placed,
        out_specs=(P(("section", "dp"), None), P(("section", "dp"), None)),
        check_vma=False,
    )
```

profile of v0, /device:TPU:1, one launch (start us, length us, event | category | flops | bytes accessed | tf_op | source)
XLA Modules:
  0.0 565.6 jit_solution(17340188780659672107)
XLA Ops:
  7.2 4.7 collective-permute-start
  12.0 5.5 collective-permute-start.1
  19.5 5.2 while.30
  19.5 1.3 compare_and_fusion.6
  22.1 1.4 convolution_bitcast_fusion.6
  25.8 1.9 collective-permute-start.2
  27.7 2.4 collective-permute-start.3
  31.0 4.4 collective-permute-done.3
  36.5 8.2 %while.31 = (s32[]{:T(128)}, f32[2,128,512]{2,0,1:T(2,128)S(1)}, s32[]{:T(128)}, s32[1,8]{1,0:T(1,128)S(1)}, s32[]{:T(128)}, /*index=5*/s32[8]{0:T(128)S(1)}, bf...) while((s32[]{:T(128)}, f32[2,128,512]{2,0,1:T(2,128)S(1)}, s32[]{:T(128)}, ...), condition=%wide.region_3.4_spmd, body=%wide.region_2.3_spmd.sunk | while | flops 147457152 | bytes 12849497 | solution.py:49
  37.2 1.7 gather_fusion.1
  38.9 1.9 convolution_bitcast_fusion.7
  40.9 2.2 copy.55
  43.1 1.6 convolution_add_fusion.7
  45.5 1.5 fusion.47
  47.4 1.6 broadcast_in_dim.45
  49.0 9.5 %while.32 = (s32[]{:T(128)}, f32[6,128,512]{2,0,1:T(8,128)}, s32[]{:T(128)}, s32[1,8]{1,0:T(1,128)S(1)}, s32[]{:T(128)}, /*index=5*/s32[8]{0:T(128)S(1)}, bf16[2...) while((s32[]{:T(128)}, f32[6,128,512]{2,0,1:T(8,128)}, s32[]{:T(128)}, ...), condition=%wide.region_5.6_spmd, body=%wide.region_4.5_spmd.sunk | while | flops 172885184 | bytes 14946649 | solution.py:69
  50.3 1.9 convolution_bitcast_fusion.8
  52.2 2.2 copy.56
  54.4 4.0 convolution_add_fusion.8
  58.5 2.6 fusion.49
  61.1 2.1 collective-permute-start.4
  63.2 3.6 collective-permute-start.5
  67.2 1.7 collective-permute-done.4
  72.0 483.5 %all-reduce.3.cloned.1.call-done = f32[512,640]{0,1:T(8,128)} async-done(((f32[512,640]{0,1:T(8,128)}), f32[512,640]{0,1:T(8,128)}) %all-reduce.3.cloned.1.call-update) | async-done | bytes 1310736
  (54 shorter events, 16.5 us)
Async XLA Ops:
  7.2 38.3 %copy-start = (bf16[512,512]{1,0:T(8,128)(2,1)S(1)}, bf16[512,512]{1,0:T(8,128)(2,1)}, u32[]{:S(2)}) copy-start(bf16[512,512]{1,0:T(8,128)(2,1)} %param.17) | copy-start | bytes 1572868
  7.2 548.3 %all-reduce.3.cloned.1.call-start = ((), (), s32[]{:S(2)}) async-start(), calls=%async_computation | async-start | bytes 2621440
  7.2 10.9 %collective-permute-start = (bf16[256,128]{1,0:T(8,128)(2,1)}, bf16[256,128]{1,0:T(8,128)(2,1)S(1)}, u32[]{:S(2)}, u32[]{:S(2)}) collective-permute-start(bf16[256,128]{1,0:T(8,128)(2,1)} %bitcast.119), channel_id=1, source_target_pairs={{0,4},{4,8},{8,12},{12,16},{16,20},{20,24},{24,28},{28,32},{32,36}... | collective-permute-start | bytes 196616 | tf_op jit(solution)/shard_map/ppermute | solution.py:12
  12.0 6.6 %collective-permute-start.1 = (bf16[256,128]{1,0:T(8,128)(2,1)}, bf16[256,128]{1,0:T(8,128)(2,1)S(1)}, u32[]{:S(2)}, u32[]{:S(2)}) collective-permute-start(bf16[256,128]{1,0:T(8,128)(2,1)} %bitcast.120), channel_id=1, source_target_pairs={{4,0},{8,4},{12,8},{16,12},{20,16},{24,20},{28,24},{32,28},{36,32}... | collective-permute-start | bytes 196616 | tf_op jit(solution)/shard_map/ppermute | solution.py:15
  19.4 5.3 copy-start.8
  19.5 4.3 copy-start.5
  24.7 11.8 %copy-start.1 = (bf16[8,128,128]{2,1,0:T(8,128)(2,1)S(1)}, bf16[8,128,128]{2,1,0:T(8,128)(2,1)}, u32[]{:S(2)}) copy-start(bf16[8,128,128]{2,1,0:T(8,128)(2,1)} %get-tuple-element.455) | copy-start | bytes 786436
  24.7 11.8 %copy-start.6 = (s32[1,8]{1,0:T(1,128)S(1)}, s32[1,8]{1,0:T(1,128)}, u32[]{:S(2)}) copy-start(s32[1,8]{1,0:T(1,128)} %get-tuple-element.467) | copy-start | bytes 100
  24.7 11.8 %copy-start.7 = (s32[8]{0:T(128)S(1)}, s32[8]{0:T(128)}, u32[]{:S(2)}) copy-start(s32[8]{0:T(128)} %get-tuple-element.469) | copy-start | bytes 100
  25.8 5.2 collective-permute-start.2
  27.7 7.7 %collective-permute-start.3 = (bf16[256,512]{1,0:T(8,128)(2,1)S(1)}, bf16[256,512]{1,0:T(8,128)(2,1)S(1)}, u32[]{:S(2)}, u32[]{:S(2)}) collective-permute-start(bf16[256,512]{1,0:T(8,128)(2,1)S(1)} %get-tuple-element.200), channel_id=1, source_target_pairs={{4,0},{8,4},{12,8},{16,12},{20,16},{24,20},{28,24},{32,28},{36,32}... | collective-permute-start | bytes 786440 | tf_op jit(solution)/shard_map/ppermute | solution.py:15
  44.8 0.7 copy-start.2
  58.5 8.3 %copy-start.3 = (bf16[2,128,512]{2,1,0:T(8,128)(2,1)S(1)}, bf16[2,128,512]{2,1,0:T(8,128)(2,1)}, u32[]{:S(2)}) copy-start(bf16[2,128,512]{2,1,0:T(8,128)(2,1)} %copy-done.2) | copy-start | bytes 786436
  61.0 9.2 %copy-start.4 = (f32[256,512]{1,0:T(8,128)S(1)}, f32[256,512]{1,0:T(8,128)}, u32[]{:S(2)}) copy-start(f32[256,512]{1,0:T(8,128)} %get-tuple-element.201) | copy-start | bytes 1572868
  61.1 7.8 %collective-permute-start.4 = (bf16[2,128,512]{2,1,0:T(8,128)(2,1)S(1)}, bf16[2,128,512]{2,1,0:T(8,128)(2,1)S(1)}, u32[]{:S(2)}, u32[]{:S(2)}) collective-permute-start(bf16[2,128,512]{2,1,0:T(8,128)(2,1)S(1)} %get-tuple-element.198), channel_id=1, source_target_pairs={{4,0},{8,4},{12,8},{16,12},{20,16},{24,20},{28,24},{32,28},{36,32}... | collective-permute-start | bytes 786440 | tf_op jit(solution)/shard_map/ppermute | solution.py:23
  63.2 6.9 %collective-permute-start.5 = (bf16[2,128,512]{2,1,0:T(8,128)(2,1)S(1)}, bf16[2,128,512]{2,1,0:T(8,128)(2,1)S(1)}, u32[]{:S(2)}, u32[]{:S(2)}) collective-permute-start(bf16[2,128,512]{2,1,0:T(8,128)(2,1)S(1)} %get-tuple-element.199), channel_id=1, source_target_pairs={{0,4},{4,8},{8,12},{12,16},{16,20},{20,24},{24,28},{28,32},{32,36}... | collective-permute-start | bytes 786440 | tf_op jit(solution)/shard_map/ppermute | solution.py:23
Sparse Core Ops, SparseCore 0:
  72.1 483.3 all-reduce.2
where the time goes:
time: 566 us
  waiting for transfers between devices  492 us (87%)
  starting transfers between devices  20.3 us (4%)
  matrix products  15.2 us (3%)
  between operations  15 us (3%)
  local copies, waits for them, and re-layouts  13.6 us (2%)
  other arithmetic  9.29 us (2%)
    unnamed x2, waiting for transfers between devices  483 us
  transfers between devices with their start and end apart: 7, of which 6 were waited for; matrix products, arithmetic and copies ran while one was open for 0% of the time, Pallas kernels for 0%

commit v1 on v0

v1 whole, which is shorter than its diff:
```python
import jax
import jax.numpy as jnp
import numpy as np
from jax import lax
from jax.experimental import pallas as pl
from jax.experimental.pallas import tpu as pltpu
from jax.sharding import Mesh
from jax.sharding import PartitionSpec as P

TILE = 128
SECTION = ("z", "y", "c")
PLANE = ("y", "c", "x")
SCALE = 0.7978845608028654
CUBIC = 0.044715
VMEM = pl.BlockSpec(memory_space=pltpu.VMEM)
SMEM = pl.BlockSpec(memory_space=pltpu.SMEM)


def fill_adjacency(rows_ref, cols_ref, count_ref, tiles_ref, adj_ref):
    adj_ref[...] = jnp.zeros_like(adj_ref)
    live = count_ref[0, 0]
    for slot in range(tiles_ref.shape[1]):

        @pl.when(slot < live)
        def _():
            row = pl.multiple_of(rows_ref[0, slot] * TILE, TILE)
            col = pl.multiple_of(cols_ref[0, slot] * TILE, TILE)
            adj_ref[pl.ds(row, TILE), pl.ds(col, TILE)] = tiles_ref[0, slot]


def dot(lhs, rhs, lhs_dim=1, rhs_dim=0):
    return lax.dot_general(
        lhs, rhs, (((lhs_dim,), (rhs_dim,)), ((), ())), preferred_element_type=jnp.float32
    )


def gelu_parts(v):
    square = v * v
    t = jnp.tanh(v * (SCALE + (SCALE * CUBIC) * square))
    half = 0.5 + 0.5 * t
    slope = half + (0.5 * v) * (1.0 - t * t) * (SCALE + (3.0 * SCALE * CUBIC) * square)
    return v * half, slope


def first_kernel(rows_ref, cols_ref, count_ref, low_ref, own_ref, high_ref, tiles_ref, out_ref, adj_ref):
    fill_adjacency(rows_ref, cols_ref, count_ref, tiles_ref, adj_ref)
    nodes = own_ref.shape[0]
    total = dot(adj_ref[:, nodes : 2 * nodes], own_ref[...])
    total += dot(adj_ref[:, :nodes], low_ref[...])
    total += dot(adj_ref[:, 2 * nodes :], high_ref[...])
    out_ref[...] = total.astype(jnp.bfloat16)


def second_kernel(
    rows_ref, cols_ref, count_ref, low_ref, own_ref, high_ref, tiles_ref, cot_ref, w1_ref, w2_ref,
    out_ref, adj_ref, agg_ref, hid_ref, slope_ref,
):
    fill_adjacency(rows_ref, cols_ref, count_ref, tiles_ref, adj_ref)
    nodes = own_ref.shape[0]
    hidden = w2_ref.shape[0]
    for part, ref in enumerate((low_ref, own_ref, high_ref)):
        place = pl.ds(part * nodes, nodes)
        agg_ref[place, :] = ref[...]
        pre1 = dot(ref[...], w1_ref[...])
        value, slope = gelu_parts(pre1)
        hid_ref[place, :] = value.astype(jnp.bfloat16)
        slope_ref[place, :] = slope
    agg2 = dot(adj_ref[...], hid_ref[...]).astype(jnp.bfloat16)
    pre2 = dot(agg2, w2_ref[...])
    unused, slope2 = gelu_parts(pre2)
    dpre2 = (cot_ref[0].astype(jnp.float32) * slope2).astype(jnp.bfloat16)
    dagg2 = dot(dpre2, w2_ref[...], 1, 1).astype(jnp.bfloat16)
    spread = dot(adj_ref[...], dagg2, 0, 0)
    dpre1 = (spread * slope_ref[...]).astype(jnp.bfloat16)
    second = dot(agg2, dpre2, 0, 0).astype(jnp.bfloat16)
    first = dot(dpre1, agg_ref[...], 0, 0).astype(jnp.bfloat16)
    groups, depth = out_ref.shape[0], out_ref.shape[1]
    target = lax.broadcasted_iota(jnp.int32, (hidden, hidden), 0)
    source = lax.broadcasted_iota(jnp.int32, (hidden, hidden), 1)
    wanted = (target % depth) * groups + target // depth
    order = (source == wanted).astype(jnp.bfloat16)
    features = first.shape[1]
    moved = dot(order, first).astype(jnp.bfloat16)
    out_ref[:, :, :features] = moved.reshape(groups, depth, features)
    moved = dot(order, second).astype(jnp.bfloat16)
    out_ref[:, :, features:] = moved.reshape(groups, depth, second.shape[1])


def plane_sum_kernel(in_ref, out_ref):
    total = in_ref[0].astype(jnp.float32)
    for source in range(1, in_ref.shape[0]):
        total += in_ref[source].astype(jnp.float32)
    out_ref[...] = jnp.zeros_like(out_ref)
    for piece in range(total.shape[1] // 128):
        out_ref[:, piece, :] = total[:, piece * 128 : (piece + 1) * 128]


def depth_sum_kernel(in_ref, first_ref, second_ref):
    total = jnp.sum(in_ref[...], axis=0)
    first_ref[...] = total[0:1, :]
    for piece in range(second_ref.shape[1] // 128):
        second_ref[:, piece * 128 : (piece + 1) * 128] = total[piece + 1 : piece + 2, :]


def shifted(block, distance):
    devices = range(lax.axis_size(SECTION))
    route = [(i, i + distance) for i in devices if i + distance in devices]
    return lax.ppermute(block, SECTION, route)


def body(features, grad_out, w_first, w_second, tile_values, tile_rows, tile_cols, tile_count):
    own = features[0]
    nodes, in_features = own.shape
    hidden = w_second.shape[0]
    depth = lax.axis_size("z")
    plane = lax.axis_size(PLANE)
    ids = (tile_rows, tile_cols, tile_count)
    adjacency = pltpu.VMEM((nodes, 3 * nodes), jnp.bfloat16)

    agg1 = pl.pallas_call(
        first_kernel,
        out_shape=jax.ShapeDtypeStruct((nodes, in_features), jnp.bfloat16),
        in_specs=[SMEM] * 3 + [VMEM] * 4,
        out_specs=VMEM,
        scratch_shapes=[adjacency],
        name="first_aggregation",
    )(*ids, shifted(own, 1), own, shifted(own, -1), tile_values)

    gradients = pl.pallas_call(
        second_kernel,
        out_shape=jax.ShapeDtypeStruct((plane, depth, in_features + hidden), jnp.bfloat16),
        in_specs=[SMEM] * 3 + [VMEM] * 7,
        out_specs=VMEM,
        scratch_shapes=[
            adjacency,
            pltpu.VMEM((3 * nodes, in_features), jnp.bfloat16),
            pltpu.VMEM((3 * nodes, hidden), jnp.bfloat16),
            pltpu.VMEM((3 * nodes, hidden), jnp.float32),
        ],
        compiler_params=pltpu.CompilerParams(vmem_limit_bytes=32 * 1024 * 1024),
        name="layers",
    )(*ids, shifted(agg1, 1), agg1, shifted(agg1, -1), tile_values, grad_out, w_first, w_second)

    gathered = lax.all_to_all(gradients, PLANE, 0, 0, tiled=True)
    partial = pl.pallas_call(
        plane_sum_kernel,
        out_shape=jax.ShapeDtypeStruct((depth, 8, 128), jnp.float32),
        in_specs=[VMEM],
        out_specs=VMEM,
        name="plane_sum",
    )(gathered)
    collected = lax.all_to_all(partial, "z", 0, 0, tiled=True)
    return pl.pallas_call(
        depth_sum_kernel,
        out_shape=(
            jax.ShapeDtypeStruct((1, in_features), jnp.float32),
            jax.ShapeDtypeStruct((1, hidden), jnp.float32),
        ),
        in_specs=[VMEM],
        out_specs=(VMEM, VMEM),
        name="depth_sum",
    )(collected)


def solution(mesh):
    fine = Mesh(mesh.devices.reshape(16, 4, 2, 4), ("z", "y", "c", "x"))
    placed = (
        P("x", SECTION, None),
        P("x", SECTION, None),
        P(),
        P(),
        P("x", SECTION, None, None),
        P("x", SECTION),
        P("x", SECTION),
        P("x", SECTION),
    )
    rows = ("z", "y", "c", "x")
    return jax.shard_map(
        body,
        mesh=fine,
        in_specs=placed,
        out_specs=(P(rows, None), P(rows, None)),
        check_vma=False,
    )
```

time: 566 us -> 82.5 us (0.15)
  waiting for transfers between devices: 492 us -> 2.55 us
  blocking collectives: 0 us -> 49 us
  matrix products: 15.2 us -> 0 us
  between operations: 15 us -> 1.38 us
  local copies, waits for them, and re-layouts: 13.6 us -> 3.43 us
  other arithmetic: 9.29 us -> 0 us
  Pallas kernels: 0 us -> 8.82 us
    unnamed x2 -> x0, waiting for transfers between devices: 483 us -> none
    all_to_all x0 -> x2, blocking collectives: none -> 49 us  [the longest x1 29.6 us: body(): collected = lax.all_to_all(partial, 'z', 0, 0, tiled=True)]
    dot_general x11 -> x0, matrix products: 15.2 us -> none  [the longest x1 4.04 us: spread_advance(): jnp.einsum('ct,tbw->cbw', onehot, product, precision=lax.Precision.HIGHEST)]
    pallas_call x0 -> x4, Pallas kernels: none -> 8.82 us  [the longest x1 3.52 us: body(): pl.pallas_call(second_kernel, out_shape=jax.ShapeDtypeStruct((plane, dept...]
    ppermute x6 -> x4, waiting for transfers between devices: 8.6 us -> 2.55 us  [shifted(): return lax.ppermute(block, SECTION, route)]
    ppermute x6 -> x4, starting transfers between devices: 20.2 us -> 16.8 us  [shifted(): return lax.ppermute(block, SECTION, route)]
  transfers between devices with their start and end apart: 7 -> 4, of which waited for: 6 -> 3; matrix products, arithmetic and copies ran while one was open for 0% -> 0% of each run, Pallas kernels for 0% -> 0%
where the time goes in v1:
time: 82.5 us; the launch traced here: 82 us
  blocking collectives  49 us (59%)
  starting transfers between devices  16.8 us (20%)
  Pallas kernels  8.82 us (11%)
  local copies, waits for them, and re-layouts  3.43 us (4%)
  waiting for transfers between devices  2.55 us (3%)
  between operations  1.38 us (2%)
    all_to_all x1, blocking collectives, body(): collected = lax.all_to_all(partial, 'z', 0, 0, tiled=True)  29.6 us
    all_to_all x1, blocking collectives, body(): gathered = lax.all_to_all(gradients, PLANE, 0, 0, tiled=True)  19.4 us
    ppermute x4, starting transfers between devices, shifted(): return lax.ppermute(block, SECTION, route)  16.8 us
    pallas_call x1, Pallas kernels, body(): pl.pallas_call(second_kernel, out_shape=jax.ShapeDtypeStruct((plane, dept...  3.52 us
    unnamed x18, local copies, waits for them, and re-layouts  3.43 us
    ppermute x4, waiting for transfers between devices, shifted(): return lax.ppermute(block, SECTION, route)  2.55 us
    pallas_call x1, Pallas kernels, body(): pl.pallas_call(first_kernel, out_shape=jax.ShapeDtypeStruct((nodes, in_fe...  2.02 us
    pallas_call x1, Pallas kernels, body(): pl.pallas_call(plane_sum_kernel, out_shape=jax.ShapeDtypeStruct((depth, 8...  1.84 us
  transfers between devices with their start and end apart: 4, of which 3 were waited for; matrix products, arithmetic and copies ran while one was open for 0% of the time, Pallas kernels for 0%

profile of v1, /device:TPU:1, one launch (start us, length us, event | category | flops | bytes accessed | tf_op | source)
XLA Modules:
  0.0 82.0 jit_solution(2663225082177662817)
XLA Ops:
  0.6 8.8 %collective-permute-start.1 = (bf16[256,128]{1,0:T(8,128)(2,1)}, bf16[256,128]{1,0:T(8,128)(2,1)S(1)}, u32[]{:S(2)}, u32[]{:S(2)}) collective-permute-start(bf16[256,128]{1,0:T(8,128)(2,1)} %bitcast.1), channel_id=1, source_target_pairs={{4,0},{8,4},{12,8},{16,12},{20,16},{24,20},{28,24},{32,28},{36,32}... | collective-permute-start | bytes 196616 | tf_op jit(solution)/shard_map/ppermute | solution.py:108
  9.4 1.9 %collective-permute-start = (bf16[256,128]{1,0:T(8,128)(2,1)}, bf16[256,128]{1,0:T(8,128)(2,1)S(1)}, u32[]{:S(2)}, u32[]{:S(2)}) collective-permute-start(bf16[256,128]{1,0:T(8,128)(2,1)} %bitcast.2), channel_id=1, source_target_pairs={{0,4},{4,8},{8,12},{12,16},{16,20},{20,24},{24,28},{28,32},{32,36}... | collective-permute-start | bytes 196616 | tf_op jit(solution)/shard_map/ppermute | solution.py:108
  12.0 0.0 copy-start
  12.0 0.0 copy-start.3
  12.0 0.0 copy-start.5
  12.0 0.0 collective-permute-done.1.high_ref
  12.1 0.9 %collective-permute-done.low_ref = bf16[256,128]{1,0:T(8,128)(2,1)S(1)} collective-permute-done((bf16[256,128]{1,0:T(8,128)(2,1)}, bf16[256,128]{1,0:T(8,128)(2,1)S(1)}, u32[]{:S(2)}, u32[]{:S(2)}) %collective-permute-start) | collective-permute-done | bytes 65568 | tf_op jit(solution)/shard_map/ppermute | solution.py:108
  13.0 0.0 copy-done.7
  13.0 0.6 copy-done.8
  13.6 2.0 %first_aggregation.1.own_ref = bf16[256,128]{1,0:T(8,128)(2,1)} custom-call(s32[1,8]{1,0:T(1,128)} %rows_ref.3, s32[1,8]{1,0:T(1,128)} %cols_ref.3, s32[1,1]{1,0:T(1,128)S(6)} %copy.10.count_ref, bf16[256,128]{1,0:T(8,128)(2,1)} %copy-done.8, bf16[256,128]{1,0:T(8,128)(2,1)} %bitcast.3, bf16[256,128]{1,0:T(8,128)(2,1)} %copy-done.7, ...), custom_call_target="tpu_custom_call" | custom-call | tf_op jit(solution)/shard_map/first_aggregation/pallas_call | solution.py:120
  15.6 2.1 %collective-permute-start.3 = (bf16[256,128]{1,0:T(8,128)(2,1)}, bf16[256,128]{1,0:T(8,128)(2,1)S(1)}, u32[]{:S(2)}, u32[]{:S(2)}) collective-permute-start(bf16[256,128]{1,0:T(8,128)(2,1)} %first_aggregation.1.own_ref), channel_id=1, source_target_pairs={{4,0},{8,4},{12,8},{16,12},{20,16},{24,20},{28,24},{32,28},{36,32}... | collective-permute-start | bytes 196616 | tf_op jit(solution)/shard_map/ppermute | solution.py:108
  17.7 4.0 %collective-permute-start.2 = (bf16[256,128]{1,0:T(8,128)(2,1)}, bf16[256,128]{1,0:T(8,128)(2,1)S(1)}, u32[]{:S(2)}, u32[]{:S(2)}) collective-permute-start(bf16[256,128]{1,0:T(8,128)(2,1)} %first_aggregation.1.own_ref), channel_id=1, source_target_pairs={{0,4},{4,8},{8,12},{12,16},{16,20},{20,24},{24,28},{28,32},{32,36}... | collective-permute-start | bytes 196616 | tf_op jit(solution)/shard_map/ppermute | solution.py:108
  21.7 0.2 collective-permute-done.3.high_ref
  21.9 1.4 %collective-permute-done.2.low_ref = bf16[256,128]{1,0:T(8,128)(2,1)S(1)} collective-permute-done((bf16[256,128]{1,0:T(8,128)(2,1)}, bf16[256,128]{1,0:T(8,128)(2,1)S(1)}, u32[]{:S(2)}, u32[]{:S(2)}) %collective-permute-start.2) | collective-permute-done | bytes 65568 | tf_op jit(solution)/shard_map/ppermute | solution.py:108
  23.3 0.0 copy-done.3
  23.4 0.0 copy-start.1
  23.4 1.0 %copy-done.1 = bf16[512,512]{1,0:T(8,128)(2,1)S(1)} copy-done((bf16[512,512]{1,0:T(8,128)(2,1)S(1)}, bf16[512,512]{1,0:T(8,128)(2,1)}, u32[]{:S(2)}) %copy-start.1) | copy-done | bytes 524312
  24.4 0.8 %copy-done.2 = bf16[256,128]{1,0:T(8,128)(2,1)S(1)} copy-done((bf16[256,128]{1,0:T(8,128)(2,1)S(1)}, bf16[256,128]{1,0:T(8,128)(2,1)}, u32[]{:S(2)}) %copy-start.2) | copy-done | bytes 65560
  25.2 0.9 %copy-done.4 = bf16[128,512]{1,0:T(8,128)(2,1)S(1)} copy-done((bf16[128,512]{1,0:T(8,128)(2,1)S(1)}, bf16[128,512]{1,0:T(8,128)(2,1)}, u32[]{:S(2)}) %copy-start.4) | copy-done | bytes 131096
  26.1 3.5 %layers.1 = bf16[32,16,640]{2,1,0:T(8,128)(2,1)S(1)} custom-call(s32[1,8]{1,0:T(1,128)S(1)} %copy-done.5, s32[1,8]{1,0:T(1,128)S(1)} %copy-done.6, s32[1,1]{1,0:T(1,128)S(6)} %copy.10.count_ref, bf16[256,128]{1,0:T(8,128)(2,1)S(1)} %collective-permute-done.2.low_ref, bf16[256,128]{1,0:T(8,128)(2,1)S(1)} %copy-done.2, ...), custom_call_target="tpu_custom_call" | custom-call | tf_op jit(solution)/shard_map/layers/pallas_call | solution.py:129
  29.7 19.4 %all_to_all.10.in_ref = bf16[32,16,640]{2,1,0:T(8,128)(2,1)} all-to-all(bf16[32,16,640]{2,1,0:T(8,128)(2,1)S(1)} %layers.1), channel_id=1, replica_groups=mesh['z'=16,'y'=4,'c'=2,'x'=4] {'y','c','x'}, dimensions={0} | all-to-all | bytes 1310720 | tf_op jit(solution)/shard_map/all_to_all | solution.py:144
  49.0 1.8 %plane_sum.1 = f32[16,8,128]{2,1,0:T(8,128)} custom-call(bf16[32,16,640]{2,1,0:T(8,128)(2,1)} %all_to_all.10.in_ref), custom_call_target="tpu_custom_call" | custom-call | tf_op jit(solution)/shard_map/plane_sum/pallas_call | solution.py:145
  50.9 29.6 %all_to_all.11.in_ref = f32[16,8,128]{2,1,0:T(8,128)} all-to-all(f32[16,8,128]{2,1,0:T(8,128)} %plane_sum.1), channel_id=1, replica_groups=mesh['z'=16,'y'=4,'c'=2,'x'=4] {'z'}, dimensions={0} | all-to-all | bytes 131072 | tf_op jit(solution)/shard_map/all_to_all | solution.py:152
  80.5 1.4 %depth_sum.1 = (f32[1,128]{1,0:T(1,128)}, f32[1,512]{1,0:T(1,128)}) custom-call(f32[16,8,128]{2,1,0:T(8,128)} %all_to_all.11.in_ref), custom_call_target="tpu_custom_call" | custom-call | tf_op jit(solution)/shard_map/depth_sum/pallas_call | solution.py:153
  (8 shorter events, 0.0 us)
Async XLA Ops:
  0.6 11.4 %collective-permute-start.1 = (bf16[256,128]{1,0:T(8,128)(2,1)}, bf16[256,128]{1,0:T(8,128)(2,1)S(1)}, u32[]{:S(2)}, u32[]{:S(2)}) collective-permute-start(bf16[256,128]{1,0:T(8,128)(2,1)} %bitcast.1), channel_id=1, source_target_pairs={{4,0},{8,4},{12,8},{16,12},{20,16},{24,20},{28,24},{32,28},{36,32}... | collective-permute-start | bytes 196616 | tf_op jit(solution)/shard_map/ppermute | solution.py:108
  9.4 3.6 %collective-permute-start = (bf16[256,128]{1,0:T(8,128)(2,1)}, bf16[256,128]{1,0:T(8,128)(2,1)S(1)}, u32[]{:S(2)}, u32[]{:S(2)}) collective-permute-start(bf16[256,128]{1,0:T(8,128)(2,1)} %bitcast.2), channel_id=1, source_target_pairs={{0,4},{4,8},{8,12},{12,16},{16,20},{20,24},{24,28},{28,32},{32,36}... | collective-permute-start | bytes 196616 | tf_op jit(solution)/shard_map/ppermute | solution.py:108
  12.0 11.3 %copy-start = (bf16[1,8,128,128]{3,2,1,0:T(8,128)(2,1)S(1)}, bf16[1,8,128,128]{3,2,1,0:T(8,128)(2,1)}, u32[]{:S(2)}) copy-start(bf16[1,8,128,128]{3,2,1,0:T(8,128)(2,1)} %tiles_ref.3) | copy-start | bytes 786436
  12.0 11.3 %copy-start.3 = (bf16[1,256,512]{2,1,0:T(8,128)(2,1)S(1)}, bf16[1,256,512]{2,1,0:T(8,128)(2,1)}, u32[]{:S(2)}) copy-start(bf16[1,256,512]{2,1,0:T(8,128)(2,1)} %cot_ref.1) | copy-start | bytes 786436
  12.0 11.3 %copy-start.5 = (s32[1,8]{1,0:T(1,128)S(1)}, s32[1,8]{1,0:T(1,128)}, u32[]{:S(2)}) copy-start(s32[1,8]{1,0:T(1,128)} %rows_ref.3) | copy-start | bytes 100
  12.0 11.3 %copy-start.6 = (s32[1,8]{1,0:T(1,128)S(1)}, s32[1,8]{1,0:T(1,128)}, u32[]{:S(2)}) copy-start(s32[1,8]{1,0:T(1,128)} %cols_ref.3) | copy-start | bytes 100
  12.0 0.9 %copy-start.7 = (bf16[256,128]{1,0:T(8,128)(2,1)}, bf16[256,128]{1,0:T(8,128)(2,1)S(1)}, u32[]{:S(2)}) copy-start(bf16[256,128]{1,0:T(8,128)(2,1)S(1)} %collective-permute-done.1.high_ref) | copy-start | bytes 196612
  13.0 0.6 copy-start.8
  15.6 6.3 %collective-permute-start.3 = (bf16[256,128]{1,0:T(8,128)(2,1)}, bf16[256,128]{1,0:T(8,128)(2,1)S(1)}, u32[]{:S(2)}, u32[]{:S(2)}) collective-permute-start(bf16[256,128]{1,0:T(8,128)(2,1)} %first_aggregation.1.own_ref), channel_id=1, source_target_pairs={{4,0},{8,4},{12,8},{16,12},{20,16},{24,20},{28,24},{32,28},{36,32}... | collective-permute-start | bytes 196616 | tf_op jit(solution)/shard_map/ppermute | solution.py:108
  17.7 5.6 %collective-permute-start.2 = (bf16[256,128]{1,0:T(8,128)(2,1)}, bf16[256,128]{1,0:T(8,128)(2,1)S(1)}, u32[]{:S(2)}, u32[]{:S(2)}) collective-permute-start(bf16[256,128]{1,0:T(8,128)(2,1)} %first_aggregation.1.own_ref), channel_id=1, source_target_pairs={{0,4},{4,8},{8,12},{12,16},{16,20},{20,24},{24,28},{28,32},{32,36}... | collective-permute-start | bytes 196616 | tf_op jit(solution)/shard_map/ppermute | solution.py:108
  23.4 1.0 %copy-start.1 = (bf16[512,512]{1,0:T(8,128)(2,1)S(1)}, bf16[512,512]{1,0:T(8,128)(2,1)}, u32[]{:S(2)}) copy-start(bf16[512,512]{1,0:T(8,128)(2,1)} %w2_ref.1) | copy-start | bytes 1572868
  24.4 0.8 %copy-start.2 = (bf16[256,128]{1,0:T(8,128)(2,1)S(1)}, bf16[256,128]{1,0:T(8,128)(2,1)}, u32[]{:S(2)}) copy-start(bf16[256,128]{1,0:T(8,128)(2,1)} %first_aggregation.1.own_ref) | copy-start | bytes 196612
  25.2 0.9 %copy-start.4 = (bf16[128,512]{1,0:T(8,128)(2,1)S(1)}, bf16[128,512]{1,0:T(8,128)(2,1)}, u32[]{:S(2)}) copy-start(bf16[128,512]{1,0:T(8,128)(2,1)} %w1_ref.1) | copy-start | bytes 393220

commit v2 on v1

v2 whole, which is shorter than its diff:
```python
import jax
import jax.numpy as jnp
from jax import lax
from jax.experimental import pallas as pl
from jax.experimental.pallas import tpu as pltpu
from jax.sharding import Mesh
from jax.sharding import PartitionSpec as P

TILE = 128
SECTION = ("z", "y", "c")
PLANE = ("y", "c", "x")
SCALE = 0.7978845608028654
CUBIC = 0.044715
VMEM = pl.BlockSpec(memory_space=pltpu.VMEM)
SMEM = pl.BlockSpec(memory_space=pltpu.SMEM)


def dot(lhs, rhs, lhs_dim=1, rhs_dim=0):
    return lax.dot_general(
        lhs, rhs, (((lhs_dim,), (rhs_dim,)), ((), ())), preferred_element_type=jnp.float32
    )


def gelu_parts(v):
    square = v * v
    t = jnp.tanh(v * (SCALE + (SCALE * CUBIC) * square))
    half = 0.5 + 0.5 * t
    slope = half + (0.5 * v) * (1.0 - t * t) * (SCALE + (3.0 * SCALE * CUBIC) * square)
    return v * half, slope


def adjacency_kernel(rows_ref, cols_ref, count_ref, odd_ref, tiles_ref, adj_ref):
    adj_ref[...] = jnp.zeros_like(adj_ref)
    live = count_ref[0, 0]
    odd = odd_ref[0]
    for slot in range(tiles_ref.shape[1]):

        @pl.when(slot < live)
        def _():
            row = pl.multiple_of(rows_ref[0, slot] * TILE, TILE)
            col = cols_ref[0, slot]
            side = col // 2
            part = jnp.where(odd == 1, 2 - side, side)
            col = pl.multiple_of((col - 2 * side) * TILE, TILE)
            adj_ref[part, pl.ds(row, TILE), pl.ds(col, TILE)] = tiles_ref[0, slot]


def layers_kernel(adj_ref, cross_ref, own_ref, other_ref, cot_ref, w1_ref, w2_ref, out_ref, slope_ref):
    hidden = w2_ref.shape[0]
    parts = (cross_ref, own_ref, other_ref)
    agg2 = None
    for part, ref in enumerate(parts):
        value, slope = gelu_parts(dot(ref[...], w1_ref[...]))
        slope_ref[part] = slope
        term = dot(adj_ref[part], value.astype(jnp.bfloat16))
        agg2 = term if agg2 is None else agg2 + term
    agg2 = agg2.astype(jnp.bfloat16)
    unused, slope2 = gelu_parts(dot(agg2, w2_ref[...]))
    dpre2 = (cot_ref[0].astype(jnp.float32) * slope2).astype(jnp.bfloat16)
    dagg2 = dot(dpre2, w2_ref[...], 1, 1).astype(jnp.bfloat16)
    first = None
    for part, ref in enumerate(parts):
        spread = dot(adj_ref[part], dagg2, 0, 0)
        dpre1 = (spread * slope_ref[part]).astype(jnp.bfloat16)
        term = dot(ref[...], dpre1, 0, 0)
        first = term if first is None else first + term
    first = first.astype(jnp.bfloat16)
    second = dot(agg2, dpre2, 0, 0).astype(jnp.bfloat16)
    groups, depth = out_ref.shape[0], out_ref.shape[1]
    target = lax.broadcasted_iota(jnp.int32, (hidden, hidden), 0)
    source = lax.broadcasted_iota(jnp.int32, (hidden, hidden), 1)
    wanted = (target % depth) * groups + target // depth
    order = (source == wanted).astype(jnp.bfloat16)
    features = first.shape[0]
    moved = dot(order, first, 1, 1).astype(jnp.bfloat16)
    out_ref[:, :, :features] = moved.reshape(groups, depth, features)
    moved = dot(order, second).astype(jnp.bfloat16)
    out_ref[:, :, features:] = moved.reshape(groups, depth, second.shape[1])


def cross_swap(block):
    count = lax.axis_size(SECTION)
    pairs = [(i, i + 1) for i in range(1, count - 1, 2)]
    return lax.ppermute(block, SECTION, pairs + [(j, i) for i, j in pairs])


def core_swap(block):
    return lax.ppermute(block, "c", [(0, 1), (1, 0)])


def body(features, grad_out, w_first, w_second, tile_values, tile_rows, tile_cols, tile_count):
    own = features[0]
    nodes, in_features = own.shape
    hidden = w_second.shape[0]
    depth = lax.axis_size("z")
    plane = lax.axis_size(PLANE)
    odd = lax.axis_index("c").astype(jnp.int32).reshape(1)

    cross = cross_swap(own)
    other = core_swap(own)
    adjacency = pl.pallas_call(
        adjacency_kernel,
        out_shape=jax.ShapeDtypeStruct((3, nodes, nodes), jnp.bfloat16),
        in_specs=[SMEM] * 4 + [VMEM],
        out_specs=VMEM,
        compiler_params=pltpu.CompilerParams(vmem_limit_bytes=4 * 1024 * 1024),
        name="adjacency",
    )(tile_rows, tile_cols, tile_count, odd, tile_values)
    near = dot(adjacency[1], own) + dot(adjacency[2], other)
    agg1 = (near + dot(adjacency[0], cross)).astype(jnp.bfloat16)

    gradients = pl.pallas_call(
        layers_kernel,
        out_shape=jax.ShapeDtypeStruct((plane, depth, in_features + hidden), jnp.bfloat16),
        in_specs=[VMEM] * 7,
        out_specs=VMEM,
        scratch_shapes=[pltpu.VMEM((3, nodes, hidden), jnp.float32)],
        compiler_params=pltpu.CompilerParams(vmem_limit_bytes=14 * 1024 * 1024),
        name="layers",
    )(adjacency, cross_swap(agg1), agg1, core_swap(agg1), grad_out, w_first, w_second)

    gathered = lax.all_to_all(gradients, PLANE, 0, 0, tiled=True)
    partial = jnp.sum(gathered.astype(jnp.float32), axis=0)
    partial = partial.reshape(depth, (in_features + hidden) // 128, 128)
    collected = lax.all_to_all(partial, "z", 0, 0, tiled=True)
    total = jnp.sum(collected, axis=0)
    first_rows = in_features // 128
    return total[:first_rows].reshape(1, in_features), total[first_rows:].reshape(1, hidden)


def solution(mesh):
    fine = Mesh(mesh.devices.reshape(16, 4, 2, 4), ("z", "y", "c", "x"))
    placed = (
        P("x", SECTION, None),
        P("x", SECTION, None),
        P(),
        P(),
        P("x", SECTION, None, None),
        P("x", SECTION),
        P("x", SECTION),
        P("x", SECTION),
    )
    rows = ("z", "y", "c", "x")
    return jax.shard_map(
        body,
        mesh=fine,
        in_specs=placed,
        out_specs=(P(rows, None), P(rows, None)),
        check_vma=False,
    )
```

time: 82.5 us -> 73.2 us (0.89)
  Pallas kernels: 8.82 us -> 3.77 us
  blocking collectives: 49 us -> 45.3 us
    pallas_call x4 -> x2, Pallas kernels: 8.82 us -> 3.77 us  [the longest x1 3.08 us: body(): pl.pallas_call(layers_kernel, out_shape=jax.ShapeDtypeStruct((plane, dept...]
    all_to_all x1, blocking collectives: 29.6 us -> 27.4 us  [body(): collected = lax.all_to_all(partial, 'z', 0, 0, tiled=True)]
    all_to_all x1, blocking collectives: 19.4 us -> 17.9 us  [body(): gathered = lax.all_to_all(gradients, PLANE, 0, 0, tiled=True)]
    slice x0 -> x2, local copies, waits for them, and re-layouts: none -> 1.09 us  [the longest x1 0.58 us: body(): total[first_rows:].reshape(1, hidden)]
    unnamed x18 -> x14, local copies, waits for them, and re-layouts: 3.43 us -> 2.41 us
  transfers between devices with their start and end apart: 4 -> 4, of which waited for: 3 -> 1; matrix products, arithmetic and copies ran while one was open for 0% -> 0% of each run, Pallas kernels for 0% -> 1%
where the time goes in v2:
time: 73.2 us; the launch traced here: 72.8 us
  blocking collectives  45.3 us (62%)
  starting transfers between devices  16.3 us (22%)
  Pallas kernels  3.77 us (5%)
  local copies, waits for them, and re-layouts  3.51 us (5%)
  waiting for transfers between devices  1.94 us (3%)
  between operations  1.4 us (2%)
    all_to_all x1, blocking collectives, body(): collected = lax.all_to_all(partial, 'z', 0, 0, tiled=True)  27.4 us
    all_to_all x1, blocking collectives, body(): gathered = lax.all_to_all(gradients, PLANE, 0, 0, tiled=True)  17.9 us
    ppermute x2, starting transfers between devices, core_swap(): return lax.ppermute(block, 'c', [(0, 1), (1, 0)])  10.7 us
    ppermute x2, starting transfers between devices, cross_swap(): return lax.ppermute(block, SECTION, pairs + [(j, i) for i, j in pairs])  5.56 us
    pallas_call x1, Pallas kernels, body(): pl.pallas_call(layers_kernel, out_shape=jax.ShapeDtypeStruct((plane, dept...  3.08 us
    unnamed x14, local copies, waits for them, and re-layouts  2.41 us
    ppermute x2, waiting for transfers between devices, cross_swap(): return lax.ppermute(block, SECTION, pairs + [(j, i) for i, j in pairs])  1.93 us
  transfers between devices with their start and end apart: 4, of which 1 were waited for; matrix products, arithmetic and copies ran while one was open for 0% of the time, Pallas kernels for 1%

profile of v2, /device:TPU:1, one launch (start us, length us, event | category | flops | bytes accessed | tf_op | source)
XLA Modules:
  0.0 72.8 jit_solution(14084525970395805996)
XLA Ops:
  0.6 8.8 %collective-permute-start = (bf16[256,128]{1,0:T(8,128)(2,1)}, bf16[256,128]{1,0:T(8,128)(2,1)S(1)}, u32[]{:S(2)}, u32[]{:S(2)}) collective-permute-start(bf16[256,128]{1,0:T(8,128)(2,1)} %bitcast.16), channel_id=1, source_target_pairs={{0,4},{4,0},{1,5},{5,1},{2,6},{6,2},{3,7},{7,3},{8,12},{12,8},{9,1... | collective-permute-start | bytes 196616 | tf_op jit(solution)/shard_map/ppermute | solution.py:88
  9.4 1.9 %collective-permute-start.1 = (bf16[256,128]{1,0:T(8,128)(2,1)}, bf16[256,128]{1,0:T(8,128)(2,1)S(1)}, u32[]{:S(2)}, u32[]{:S(2)}) collective-permute-start(bf16[256,128]{1,0:T(8,128)(2,1)} %bitcast.17), channel_id=1, source_target_pairs={{4,8},{12,16},{20,24},{28,32},{36,40},{44,48},{52,56},{60,64},{68,... | collective-permute-start | bytes 196616 | tf_op jit(solution)/shard_map/ppermute | solution.py:84
  12.0 0.0 copy-start.2
  12.0 0.9 %copy-done.2 = bf16[1,8,128,128]{3,2,1,0:T(8,128)(2,1)S(1)} copy-done((bf16[1,8,128,128]{3,2,1,0:T(8,128)(2,1)S(1)}, bf16[1,8,128,128]{3,2,1,0:T(8,128)(2,1)}, u32[]{:S(2)}) %copy-start.2) | copy-done | bytes 262168
  13.0 0.7 copy-done.4
  13.6 0.7 copy-done.5
  14.3 0.7 adjacency.1.adj_ref
  15.0 0.1 copy-done.6
  15.1 0.2 fusion.1
  15.3 0.0 collective-permute-done
  15.3 0.2 convolution_add_fusion.1
  15.5 0.0 collective-permute-done.1
  15.5 0.2 fusion.own_ref
  15.7 1.9 %collective-permute-start.3 = (bf16[256,128]{1,0:T(8,128)(2,1)S(1)}, bf16[256,128]{1,0:T(8,128)(2,1)S(1)}, u32[]{:S(2)}, u32[]{:S(2)}) collective-permute-start(bf16[256,128]{1,0:T(8,128)(2,1)S(1)} %fusion.own_ref), channel_id=1, source_target_pairs={{0,4},{4,0},{1,5},{5,1},{2,6},{6,2},{3,7},{7,3},{8,12},{12,8},{9,1... | collective-permute-start | bytes 196616 | tf_op jit(solution)/shard_map/ppermute | solution.py:88
  17.6 3.6 %collective-permute-start.2 = (bf16[256,128]{1,0:T(8,128)(2,1)S(1)}, bf16[256,128]{1,0:T(8,128)(2,1)S(1)}, u32[]{:S(2)}, u32[]{:S(2)}) collective-permute-start(bf16[256,128]{1,0:T(8,128)(2,1)S(1)} %fusion.own_ref), channel_id=1, source_target_pairs={{4,8},{12,16},{20,24},{28,32},{36,40},{44,48},{52,56},{60,64},{68,... | collective-permute-start | bytes 196616 | tf_op jit(solution)/shard_map/ppermute | solution.py:84
  21.2 0.0 collective-permute-done.3.other_ref
  21.2 1.9 %collective-permute-done.2.cross_ref = bf16[256,128]{1,0:T(8,128)(2,1)S(1)} collective-permute-done((bf16[256,128]{1,0:T(8,128)(2,1)S(1)}, bf16[256,128]{1,0:T(8,128)(2,1)S(1)}, u32[]{:S(2)}, u32[]{:S(2)}) %collective-permute-start.2) | collective-permute-done | bytes 65568 | tf_op jit(solution)/shard_map/ppermute | solution.py:84
  23.2 0.0 copy-done
  23.2 3.1 %layers.1 = bf16[32,16,640]{2,1,0:T(8,128)(2,1)S(1)} custom-call(bf16[3,256,256]{2,1,0:T(8,128)(2,1)S(1)} %adjacency.1.adj_ref, bf16[256,128]{1,0:T(8,128)(2,1)S(1)} %collective-permute-done.2.cross_ref, bf16[256,128]{1,0:T(8,128)(2,1)S(1)} %fusion.own_ref, bf16[256,128]{1,0:T(8,128)(2,1)S(1)} %collective-permute-done.3.other_ref, ...), custom_call_target="tpu_custom_call" | custom-call | tf_op jit(solution)/shard_map/layers/pallas_call | solution.py:112
  26.3 17.9 %all_to_all.10 = bf16[32,16,640]{2,1,0:T(8,128)(2,1)S(1)} all-to-all(bf16[32,16,640]{2,1,0:T(8,128)(2,1)S(1)} %layers.1), channel_id=1, replica_groups=mesh['z'=16,'y'=4,'c'=2,'x'=4] {'y','c','x'}, dimensions={0} | all-to-all | bytes 1310720 | tf_op jit(solution)/shard_map/all_to_all | solution.py:122
  44.2 0.1 convert_reduce_fusion
  44.3 27.4 %all_to_all.11 = f32[16,5,128]{2,1,0:T(8,128)S(1)} all-to-all(f32[16,5,128]{2,1,0:T(8,128)S(1)} %reshape.14), channel_id=1, replica_groups=mesh['z'=16,'y'=4,'c'=2,'x'=4] {'z'}, dimensions={0} | all-to-all | bytes 81920 | tf_op jit(solution)/shard_map/all_to_all | solution.py:125
  71.7 0.5 slice.18
  72.2 0.6 slice.19
  (10 shorter events, 0.0 us)
Async XLA Ops:
  0.6 14.7 %collective-permute-start = (bf16[256,128]{1,0:T(8,128)(2,1)}, bf16[256,128]{1,0:T(8,128)(2,1)S(1)}, u32[]{:S(2)}, u32[]{:S(2)}) collective-permute-start(bf16[256,128]{1,0:T(8,128)(2,1)} %bitcast.16), channel_id=1, source_target_pairs={{0,4},{4,0},{1,5},{5,1},{2,6},{6,2},{3,7},{7,3},{8,12},{12,8},{9,1... | collective-permute-start | bytes 196616 | tf_op jit(solution)/shard_map/ppermute | solution.py:88
  9.4 6.0 %collective-permute-start.1 = (bf16[256,128]{1,0:T(8,128)(2,1)}, bf16[256,128]{1,0:T(8,128)(2,1)S(1)}, u32[]{:S(2)}, u32[]{:S(2)}) collective-permute-start(bf16[256,128]{1,0:T(8,128)(2,1)} %bitcast.17), channel_id=1, source_target_pairs={{4,8},{12,16},{20,24},{28,32},{36,40},{44,48},{52,56},{60,64},{68,... | collective-permute-start | bytes 196616 | tf_op jit(solution)/shard_map/ppermute | solution.py:84
  12.0 1.0 %copy-start.2 = (bf16[1,8,128,128]{3,2,1,0:T(8,128)(2,1)S(1)}, bf16[1,8,128,128]{3,2,1,0:T(8,128)(2,1)}, u32[]{:S(2)}) copy-start(bf16[1,8,128,128]{3,2,1,0:T(8,128)(2,1)} %tiles_ref.1) | copy-start | bytes 786436
  13.0 0.7 copy-start.4
  13.6 0.7 copy-start.5
  14.3 0.8 %copy-start.6 = (bf16[1,256,128]{2,1,0:T(8,128)(2,1)S(1)}, bf16[1,256,128]{2,1,0:T(8,128)(2,1)}, u32[]{:S(2)}) copy-start(bf16[1,256,128]{2,1,0:T(8,128)(2,1)} %param.8) | copy-start | bytes 196612
  15.1 8.1 %copy-start = (bf16[512,512]{1,0:T(8,128)(2,1)S(1)}, bf16[512,512]{1,0:T(8,128)(2,1)}, u32[]{:S(2)}) copy-start(bf16[512,512]{1,0:T(8,128)(2,1)} %w2_ref.1) | copy-start | bytes 1572868
  15.1 8.1 %copy-start.1 = (bf16[1,256,512]{2,1,0:T(8,128)(2,1)S(1)}, bf16[1,256,512]{2,1,0:T(8,128)(2,1)}, u32[]{:S(2)}) copy-start(bf16[1,256,512]{2,1,0:T(8,128)(2,1)} %cot_ref.1) | copy-start | bytes 786436
  15.1 8.1 %copy-start.3 = (bf16[128,512]{1,0:T(8,128)(2,1)S(1)}, bf16[128,512]{1,0:T(8,128)(2,1)}, u32[]{:S(2)}) copy-start(bf16[128,512]{1,0:T(8,128)(2,1)} %w1_ref.1) | copy-start | bytes 393220
  15.7 5.6 %collective-permute-start.3 = (bf16[256,128]{1,0:T(8,128)(2,1)S(1)}, bf16[256,128]{1,0:T(8,128)(2,1)S(1)}, u32[]{:S(2)}, u32[]{:S(2)}) collective-permute-start(bf16[256,128]{1,0:T(8,128)(2,1)S(1)} %fusion.own_ref), channel_id=1, source_target_pairs={{0,4},{4,0},{1,5},{5,1},{2,6},{6,2},{3,7},{7,3},{8,12},{12,8},{9,1... | collective-permute-start | bytes 196616 | tf_op jit(solution)/shard_map/ppermute | solution.py:88
  17.6 5.6 %collective-permute-start.2 = (bf16[256,128]{1,0:T(8,128)(2,1)S(1)}, bf16[256,128]{1,0:T(8,128)(2,1)S(1)}, u32[]{:S(2)}, u32[]{:S(2)}) collective-permute-start(bf16[256,128]{1,0:T(8,128)(2,1)S(1)} %fusion.own_ref), channel_id=1, source_target_pairs={{4,8},{12,16},{20,24},{28,32},{36,40},{44,48},{52,56},{60,64},{68,... | collective-permute-start | bytes 196616 | tf_op jit(solution)/shard_map/ppermute | solution.py:84

commit v3 on v2

v3 whole, which is shorter than its diff:
```python
import functools

import jax
import jax.numpy as jnp
from jax import lax
from jax.experimental import pallas as pl
from jax.experimental.pallas import tpu as pltpu
from jax.sharding import Mesh
from jax.sharding import PartitionSpec as P

TILE = 128
SECTION = ("z", "y", "c")
PLANE = ("y", "c", "x")
SCALE = 0.7978845608028654
CUBIC = 0.044715
MIB = 1024 * 1024
VMEM = pl.BlockSpec(memory_space=pltpu.VMEM)
HBM = pl.BlockSpec(memory_space=pltpu.HBM)
SMEM = pl.BlockSpec(memory_space=pltpu.SMEM)


def dot(lhs, rhs, lhs_dim=1, rhs_dim=0):
    return lax.dot_general(
        lhs, rhs, (((lhs_dim,), (rhs_dim,)), ((), ())), preferred_element_type=jnp.float32
    )


def gelu_parts(v):
    square = v * v
    t = jnp.tanh(v * (SCALE + (SCALE * CUBIC) * square))
    half = 0.5 + 0.5 * t
    slope = half + (0.5 * v) * (1.0 - t * t) * (SCALE + (3.0 * SCALE * CUBIC) * square)
    return v * half, slope


def adjacency_kernel(
    odd_ref, count_ref, rows_hbm, cols_hbm, tiles_hbm, own_hbm, adj_ref, near_ref,
    rows_ref, cols_ref, tiles_ref, own_ref, sems,
):
    pairs = ((rows_hbm, rows_ref), (cols_hbm, cols_ref), (tiles_hbm, tiles_ref), (own_hbm, own_ref))
    copies = [pltpu.make_async_copy(src, dst, sems.at[i]) for i, (src, dst) in enumerate(pairs)]
    for copy in copies:
        copy.start()
    adj_ref[...] = jnp.zeros_like(adj_ref)
    odd = odd_ref[0]
    for copy in copies:
        copy.wait()
    live = count_ref[0, 0]
    for slot in range(tiles_ref.shape[1]):

        @pl.when(slot < live)
        def _():
            row = pl.multiple_of(rows_ref[0, slot] * TILE, TILE)
            col = cols_ref[0, slot]
            side = col // 2
            part = jnp.where(odd == 1, 2 - side, side)
            col = pl.multiple_of((col - 2 * side) * TILE, TILE)
            adj_ref[part, pl.ds(row, TILE), pl.ds(col, TILE)] = tiles_ref[0, slot]

    near_ref[...] = dot(adj_ref[1], own_ref[0])


def own_kernel(adj_ref, own_ref, w1_ref, w2_ref, agg2_ref, slope_ref, w1_out, w2_out, *, groups):
    hidden = w2_ref.shape[0]
    depth = hidden // groups
    target = lax.broadcasted_iota(jnp.int32, (hidden, hidden), 0)
    source = lax.broadcasted_iota(jnp.int32, (hidden, hidden), 1)
    order = (source == (target % depth) * groups + target // depth).astype(jnp.bfloat16)
    w1 = dot(w1_ref[...], order, 1, 1).astype(jnp.bfloat16)
    w1_out[...] = w1
    w2_out[...] = dot(order, w2_ref[...]).astype(jnp.bfloat16)
    value, slope = gelu_parts(dot(own_ref[...], w1))
    slope_ref[...] = slope
    agg2_ref[...] = dot(adj_ref[1], value.astype(jnp.bfloat16))


def cross_kernel(adj_ref, cross_ref, w1_ref, near_ref, agg2_ref, slope_ref):
    value, slope = gelu_parts(dot(cross_ref[...], w1_ref[...]))
    slope_ref[...] = slope
    agg2_ref[...] = near_ref[...] + dot(adj_ref[0], value.astype(jnp.bfloat16))


def layers_kernel(
    adj_ref, cross_ref, own_ref, other_ref, cot_ref, agg2_ref, own_slope_ref, cross_slope_ref, w1_ref, w2_ref, out_ref
):
    value, slope = gelu_parts(dot(other_ref[...], w1_ref[...]))
    agg2 = agg2_ref[...] + dot(adj_ref[2], value.astype(jnp.bfloat16))
    agg2 = agg2.astype(jnp.bfloat16)
    unused, slope2 = gelu_parts(dot(agg2, w2_ref[...]))
    dpre2 = (cot_ref[0].astype(jnp.float32) * slope2).astype(jnp.bfloat16)
    dagg2 = dot(dpre2, w2_ref[...], 1, 1).astype(jnp.bfloat16)
    first = None
    parts = ((cross_ref, cross_slope_ref[...]), (own_ref, own_slope_ref[...]), (other_ref, slope))
    for part, (ref, slope) in enumerate(parts):
        spread = dot(adj_ref[part], dagg2, 0, 0)
        dpre1 = (spread * slope).astype(jnp.bfloat16)
        term = dot(ref[...], dpre1, 0, 0)
        first = term if first is None else first + term
    second = dot(agg2, dpre2, 0, 0)
    groups, depth = out_ref.shape[0], out_ref.shape[1]
    features = first.shape[0]
    out_ref[:, :, :features] = first.T.astype(jnp.bfloat16).reshape(groups, depth, features)
    out_ref[:, :, features:] = second.astype(jnp.bfloat16).reshape(groups, depth, second.shape[1])


def depth_sum_kernel(in_ref, first_ref, second_ref):
    total = jnp.sum(in_ref[...], axis=0)
    pieces = first_ref.shape[1] // 128
    for piece in range(total.shape[0]):
        ref, place = (first_ref, piece) if piece < pieces else (second_ref, piece - pieces)
        ref[:, place * 128 : (place + 1) * 128] = total[piece : piece + 1, :]


def cross_swap(block):
    count = lax.axis_size(SECTION)
    pairs = [(i, i + 1) for i in range(1, count - 1, 2)]
    return lax.ppermute(block, SECTION, pairs + [(j, i) for i, j in pairs])


def core_swap(block):
    return lax.ppermute(block, "c", [(0, 1), (1, 0)])


def body(features, grad_out, w_first, w_second, tile_values, tile_rows, tile_cols, tile_count):
    own = features[0]
    nodes, in_features = own.shape
    hidden = w_second.shape[0]
    depth = lax.axis_size("z")
    plane = lax.axis_size(PLANE)
    odd = lax.axis_index("c").astype(jnp.int32).reshape(1)

    cross = cross_swap(own)
    other = core_swap(own)
    inputs = (tile_rows, tile_cols, tile_values, features)
    adjacency, near = pl.pallas_call(
        adjacency_kernel,
        out_shape=(
            jax.ShapeDtypeStruct((3, nodes, nodes), jnp.bfloat16),
            jax.ShapeDtypeStruct((nodes, in_features), jnp.float32),
        ),
        in_specs=[SMEM] * 2 + [HBM] * 4,
        out_specs=(VMEM, VMEM),
        scratch_shapes=[pltpu.SMEM(i.shape, i.dtype) for i in inputs[:2]]
        + [pltpu.VMEM(i.shape, i.dtype) for i in inputs[2:]]
        + [pltpu.SemaphoreType.DMA((4,))],
        compiler_params=pltpu.CompilerParams(vmem_limit_bytes=4 * MIB),
        name="adjacency",
    )(odd, tile_count, *[pltpu.with_memory_space_constraint(i, pltpu.HBM) for i in inputs])
    agg1 = near + dot(adjacency[2], other) + dot(adjacency[0], cross)
    agg1 = agg1.astype(jnp.bfloat16)

    cross = cross_swap(agg1)
    other = core_swap(agg1)
    agg2, own_slope, w_first, w_second = pl.pallas_call(
        functools.partial(own_kernel, groups=plane),
        out_shape=(
            jax.ShapeDtypeStruct((nodes, hidden), jnp.float32),
            jax.ShapeDtypeStruct((nodes, hidden), jnp.float32),
            jax.ShapeDtypeStruct(w_first.shape, w_first.dtype),
            jax.ShapeDtypeStruct(w_second.shape, w_second.dtype),
        ),
        in_specs=[VMEM] * 4,
        out_specs=[VMEM] * 4,
        compiler_params=pltpu.CompilerParams(vmem_limit_bytes=12 * MIB),
        cost_estimate=pl.CostEstimate(flops=600_000_000, bytes_accessed=4 * MIB, transcendentals=131072),
        name="own_part",
    )(adjacency, agg1, w_first, w_second)
    agg2, cross_slope = pl.pallas_call(
        cross_kernel,
        out_shape=(
            jax.ShapeDtypeStruct((nodes, hidden), jnp.float32),
            jax.ShapeDtypeStruct((nodes, hidden), jnp.float32),
        ),
        in_specs=[VMEM] * 4,
        out_specs=[VMEM] * 2,
        compiler_params=pltpu.CompilerParams(vmem_limit_bytes=8 * MIB),
        name="cross_part",
    )(adjacency, cross, w_first, agg2)
    gradients = pl.pallas_call(
        layers_kernel,
        out_shape=jax.ShapeDtypeStruct((plane, depth, in_features + hidden), jnp.bfloat16),
        in_specs=[VMEM] * 10,
        out_specs=VMEM,
        compiler_params=pltpu.CompilerParams(vmem_limit_bytes=12 * MIB),
        name="layers",
    )(adjacency, cross, agg1, other, grad_out, agg2, own_slope, cross_slope, w_first, w_second)

    gathered = lax.all_to_all(gradients, PLANE, 0, 0, tiled=True)
    partial = jnp.sum(gathered.astype(jnp.float32), axis=0)
    partial = partial.reshape(depth, (in_features + hidden) // 128, 128)
    collected = lax.all_to_all(partial, "z", 0, 0, tiled=True)
    return pl.pallas_call(
        depth_sum_kernel,
        out_shape=(
            jax.ShapeDtypeStruct((1, in_features), jnp.float32),
            jax.ShapeDtypeStruct((1, hidden), jnp.float32),
        ),
        in_specs=[VMEM],
        out_specs=(VMEM, VMEM),
        compiler_params=pltpu.CompilerParams(vmem_limit_bytes=4 * MIB),
        name="depth_sum",
    )(collected)


def solution(mesh):
    fine = Mesh(mesh.devices.reshape(16, 4, 2, 4), ("z", "y", "c", "x"))
    placed = (
        P("x", SECTION, None),
        P("x", SECTION, None),
        P(),
        P(),
        P("x", SECTION, None, None),
        P("x", SECTION),
        P("x", SECTION),
        P("x", SECTION),
    )
    rows = ("z", "y", "c", "x")
    return jax.shard_map(
        body,
        mesh=fine,
        in_specs=placed,
        out_specs=(P(rows, None), P(rows, None)),
        check_vma=False,
    )
```

time: 73.2 us -> 67.9 us (0.928)
  local copies, waits for them, and re-layouts: 3.51 us -> 0.02 us
  starting transfers between devices: 16.3 us -> 13.4 us
  Pallas kernels: 3.77 us -> 5.47 us
  waiting for transfers between devices: 1.94 us -> 0.57 us
  blocking collectives: 45.3 us -> 46.2 us
    ppermute x2, starting transfers between devices: 10.7 us -> 6.78 us  [core_swap(): return lax.ppermute(block, 'c', [(0, 1), (1, 0)])]
    pallas_call x1 -> x4, Pallas kernels: 0.68 us -> 3.57 us  [the longest x1 1.21 us: body(): pl.pallas_call(adjacency_kernel, out_shape=(jax.ShapeDtypeStruct((3, node...]
    unnamed x14 -> x6, local copies, waits for them, and re-layouts: 2.41 us -> 0.01 us
    ppermute x2, waiting for transfers between devices: 1.93 us -> 0.56 us  [cross_swap(): return lax.ppermute(block, SECTION, pairs + [(j, i) for i, j in pairs])]
    pallas_call x1, Pallas kernels: 3.08 us -> 1.9 us  [body(): pl.pallas_call(layers_kernel, out_shape=jax.ShapeDtypeStruct((plane, dept...]
    slice x2 -> x0, local copies, waits for them, and re-layouts: 1.09 us -> none  [the longest x1 0.58 us: body(): total[first_rows:].reshape(1, hidden)]
    ppermute x2, starting transfers between devices: 5.56 us -> 6.65 us  [cross_swap(): return lax.ppermute(block, SECTION, pairs + [(j, i) for i, j in pairs])]
    all_to_all x1, blocking collectives: 17.9 us -> 18.8 us  [body(): gathered = lax.all_to_all(gradients, PLANE, 0, 0, tiled=True)]
  transfers between devices with their start and end apart: 4 -> 4, of which waited for: 1 -> 1; matrix products, arithmetic and copies ran while one was open for 0% -> 0% of each run, Pallas kernels for 1% -> 4%
where the time goes in v3:
time: 67.9 us; the launch traced here: 67.6 us
  blocking collectives  46.2 us (68%)
  starting transfers between devices  13.4 us (20%)
  Pallas kernels  5.47 us (8%)
  between operations  1.43 us (2%)
    all_to_all x1, blocking collectives, body(): collected = lax.all_to_all(partial, 'z', 0, 0, tiled=True)  27.4 us
    all_to_all x1, blocking collectives, body(): gathered = lax.all_to_all(gradients, PLANE, 0, 0, tiled=True)  18.8 us
    ppermute x2, starting transfers between devices, core_swap(): return lax.ppermute(block, 'c', [(0, 1), (1, 0)])  6.78 us
    ppermute x2, starting transfers between devices, cross_swap(): return lax.ppermute(block, SECTION, pairs + [(j, i) for i, j in pairs])  6.65 us
    pallas_call x1, Pallas kernels, body(): pl.pallas_call(layers_kernel, out_shape=jax.ShapeDtypeStruct((plane, dept...  1.9 us
  transfers between devices with their start and end apart: 4, of which 1 were waited for; matrix products, arithmetic and copies ran while one was open for 0% of the time, Pallas kernels for 4%

profile of v3, /device:TPU:1, one launch (start us, length us, event | category | flops | bytes accessed | tf_op | source)
XLA Modules:
  0.0 67.6 jit_solution(2098205291468822047)
XLA Ops:
  0.6 0.0 copy-start.1
  0.6 0.0 copy-start.2
  0.7 4.7 %collective-permute-start.1 = (bf16[256,128]{1,0:T(8,128)(2,1)}, bf16[256,128]{1,0:T(8,128)(2,1)S(1)}, u32[]{:S(2)}, u32[]{:S(2)}) collective-permute-start(bf16[256,128]{1,0:T(8,128)(2,1)} %bitcast.10), channel_id=1, source_target_pairs={{4,8},{12,16},{20,24},{28,32},{36,40},{44,48},{52,56},{60,64},{68,... | collective-permute-start | bytes 196616 | tf_op jit(solution)/shard_map/ppermute | solution.py:117
  5.4 4.9 %collective-permute-start = (bf16[256,128]{1,0:T(8,128)(2,1)}, bf16[256,128]{1,0:T(8,128)(2,1)S(1)}, u32[]{:S(2)}, u32[]{:S(2)}) collective-permute-start(bf16[256,128]{1,0:T(8,128)(2,1)} %bitcast.11), channel_id=1, source_target_pairs={{0,4},{4,0},{1,5},{5,1},{2,6},{6,2},{3,7},{7,3},{8,12},{12,8},{9,1... | collective-permute-start | bytes 196616 | tf_op jit(solution)/shard_map/ppermute | solution.py:121
  10.9 1.2 %adjacency.1 = (bf16[3,256,256]{2,1,0:T(8,128)(2,1)S(1)}, f32[256,128]{1,0:T(8,128)S(1)}) custom-call(s32[1]{0:T(128)} %bitcast.odd_ref, s32[1,1]{1,0:T(1,128)S(6)} %copy.10.count_ref, s32[1,8]{1,0:T(1,128)} %rows_hbm.1, s32[1,8]{1,0:T(1,128)} %cols_hbm.1, bf16[1,8,128,128]{3,2,1,0:T(8,128)(2,1)} %tiles_hbm.1, bf16[1,256,128]{2,1,0:T(8,128)(2,1)} %own_hbm.1), custom_call_target="tpu_custom_call" | custom-call | tf_op jit(solution)/shard_map/adjacency/pallas_call | solution.py:135
  12.1 0.0 collective-permute-done.1
  12.1 0.2 fusion.2
  12.3 0.0 collective-permute-done
  12.3 0.2 fusion.1.own_ref
  12.5 1.9 %collective-permute-start.2 = (bf16[256,128]{1,0:T(8,128)(2,1)S(1)}, bf16[256,128]{1,0:T(8,128)(2,1)S(1)}, u32[]{:S(2)}, u32[]{:S(2)}) collective-permute-start(bf16[256,128]{1,0:T(8,128)(2,1)S(1)} %fusion.1.own_ref), channel_id=1, source_target_pairs={{4,8},{12,16},{20,24},{28,32},{36,40},{44,48},{52,56},{60,64},{68,... | collective-permute-start | bytes 196616 | tf_op jit(solution)/shard_map/ppermute | solution.py:117
  14.4 1.9 %collective-permute-start.3 = (bf16[256,128]{1,0:T(8,128)(2,1)S(1)}, bf16[256,128]{1,0:T(8,128)(2,1)S(1)}, u32[]{:S(2)}, u32[]{:S(2)}) collective-permute-start(bf16[256,128]{1,0:T(8,128)(2,1)S(1)} %fusion.1.own_ref), channel_id=1, source_target_pairs={{0,4},{4,0},{1,5},{5,1},{2,6},{6,2},{3,7},{7,3},{8,12},{12,8},{9,1... | collective-permute-start | bytes 196616 | tf_op jit(solution)/shard_map/ppermute | solution.py:121
  16.4 0.0 copy-done.1
  16.4 0.0 copy-done.2
  16.4 1.1 %own_part.1 = (f32[256,512]{1,0:T(8,128)S(1)}, f32[256,512]{1,0:T(8,128)S(1)}, bf16[128,512]{1,0:T(8,128)(2,1)S(1)}, bf16[512,512]{1,0:T(8,128)(2,1)S(1)}) custom-call(bf16[3,256,256]{2,1,0:T(8,128)(2,1)S(1)} %get-tuple-element.10.adj_ref, bf16[256,128]{1,0:T(8,128)(2,1)S(1)} %fusion.1.own_ref, bf16[128,512]{1,0:T(8,128)(2,1)S(1)} %copy-done.2, ...), custom_call_target="tpu_custom_call" | custom-call | flops 600000000 | bytes 4194304 | tf_op jit(solution)/shard_map/own_part/pallas_call | solution.py:154
  17.5 0.0 copy-start
  17.5 0.6 collective-permute-done.2.cross_ref
  18.1 0.6 cross_part.1
  18.7 0.0 collective-permute-done.3.other_ref
  18.7 0.0 copy-done
  18.7 1.9 %layers.1 = bf16[32,16,640]{2,1,0:T(8,128)(2,1)S(1)} custom-call(bf16[3,256,256]{2,1,0:T(8,128)(2,1)S(1)} %get-tuple-element.10.adj_ref, bf16[256,128]{1,0:T(8,128)(2,1)S(1)} %collective-permute-done.2.cross_ref, bf16[256,128]{1,0:T(8,128)(2,1)S(1)} %fusion.1.own_ref, bf16[256,128]{1,0:T(8,128)(2,1)S(1)} %collective-permute-done.3.other_ref, ...), custom_call_target="tpu_custom_call" | custom-call | tf_op jit(solution)/shard_map/layers/pallas_call | solution.py:179
  20.6 18.8 %all_to_all.10 = bf16[32,16,640]{2,1,0:T(8,128)(2,1)S(1)} all-to-all(bf16[32,16,640]{2,1,0:T(8,128)(2,1)S(1)} %layers.1), channel_id=1, replica_groups=mesh['z'=16,'y'=4,'c'=2,'x'=4] {'y','c','x'}, dimensions={0} | all-to-all | bytes 1310720 | tf_op jit(solution)/shard_map/all_to_all | solution.py:188
  39.5 0.1 convert_reduce_fusion
  39.6 27.4 %all_to_all.11.in_ref = f32[16,5,128]{2,1,0:T(8,128)S(1)} all-to-all(f32[16,5,128]{2,1,0:T(8,128)S(1)} %reshape.11), channel_id=1, replica_groups=mesh['z'=16,'y'=4,'c'=2,'x'=4] {'z'}, dimensions={0} | all-to-all | bytes 81920 | tf_op jit(solution)/shard_map/all_to_all | solution.py:191
  67.0 0.6 depth_sum.1
  (1 shorter events, 0.0 us)
Async XLA Ops:
  0.6 15.7 %copy-start.1 = (bf16[512,512]{1,0:T(8,128)(2,1)S(1)}, bf16[512,512]{1,0:T(8,128)(2,1)}, u32[]{:S(2)}) copy-start(bf16[512,512]{1,0:T(8,128)(2,1)} %w2_ref.1) | copy-start | bytes 1572868
  0.6 15.7 %copy-start.2 = (bf16[128,512]{1,0:T(8,128)(2,1)S(1)}, bf16[128,512]{1,0:T(8,128)(2,1)}, u32[]{:S(2)}) copy-start(bf16[128,512]{1,0:T(8,128)(2,1)} %w1_ref.1) | copy-start | bytes 393220
  0.7 11.5 %collective-permute-start.1 = (bf16[256,128]{1,0:T(8,128)(2,1)}, bf16[256,128]{1,0:T(8,128)(2,1)S(1)}, u32[]{:S(2)}, u32[]{:S(2)}) collective-permute-start(bf16[256,128]{1,0:T(8,128)(2,1)} %bitcast.10), channel_id=1, source_target_pairs={{4,8},{12,16},{20,24},{28,32},{36,40},{44,48},{52,56},{60,64},{68,... | collective-permute-start | bytes 196616 | tf_op jit(solution)/shard_map/ppermute | solution.py:117
  5.4 6.9 %collective-permute-start = (bf16[256,128]{1,0:T(8,128)(2,1)}, bf16[256,128]{1,0:T(8,128)(2,1)S(1)}, u32[]{:S(2)}, u32[]{:S(2)}) collective-permute-start(bf16[256,128]{1,0:T(8,128)(2,1)} %bitcast.11), channel_id=1, source_target_pairs={{0,4},{4,0},{1,5},{5,1},{2,6},{6,2},{3,7},{7,3},{8,12},{12,8},{9,1... | collective-permute-start | bytes 196616 | tf_op jit(solution)/shard_map/ppermute | solution.py:121
  12.5 5.6 %collective-permute-start.2 = (bf16[256,128]{1,0:T(8,128)(2,1)S(1)}, bf16[256,128]{1,0:T(8,128)(2,1)S(1)}, u32[]{:S(2)}, u32[]{:S(2)}) collective-permute-start(bf16[256,128]{1,0:T(8,128)(2,1)S(1)} %fusion.1.own_ref), channel_id=1, source_target_pairs={{4,8},{12,16},{20,24},{28,32},{36,40},{44,48},{52,56},{60,64},{68,... | collective-permute-start | bytes 196616 | tf_op jit(solution)/shard_map/ppermute | solution.py:117
  14.4 4.3 %collective-permute-start.3 = (bf16[256,128]{1,0:T(8,128)(2,1)S(1)}, bf16[256,128]{1,0:T(8,128)(2,1)S(1)}, u32[]{:S(2)}, u32[]{:S(2)}) collective-permute-start(bf16[256,128]{1,0:T(8,128)(2,1)S(1)} %fusion.1.own_ref), channel_id=1, source_target_pairs={{0,4},{4,0},{1,5},{5,1},{2,6},{6,2},{3,7},{7,3},{8,12},{12,8},{9,1... | collective-permute-start | bytes 196616 | tf_op jit(solution)/shard_map/ppermute | solution.py:121
  17.5 1.2 %copy-start = (bf16[1,256,512]{2,1,0:T(8,128)(2,1)S(1)}, bf16[1,256,512]{2,1,0:T(8,128)(2,1)}, u32[]{:S(2)}) copy-start(bf16[1,256,512]{2,1,0:T(8,128)(2,1)} %cot_ref.1) | copy-start | bytes 786436

commit v4 on v3

--- a/solution.py
+++ b/solution.py
@@ -60,7 +60,20 @@
     near_ref[...] = dot(adj_ref[1], own_ref[0])
 
 
-def own_kernel(adj_ref, own_ref, w1_ref, w2_ref, agg2_ref, slope_ref, w1_out, w2_out, *, groups):
+def aggregate_kernel(other_ref, adj_ref, near_ref, cross_ref, agg1_ref, sent_ref):
+    nodes = agg1_ref.shape[0]
+    agg1 = near_ref[...] + dot(adj_ref[2], other_ref[...]) + dot(adj_ref[0], cross_ref[...])
+    agg1 = agg1.astype(jnp.bfloat16)
+    agg1_ref[...] = agg1
+    sent_ref[:nodes, :] = agg1
+    sent_ref[nodes:, :] = jnp.zeros((sent_ref.shape[0] - nodes, agg1.shape[1]), agg1.dtype)
+
+
+def own_kernel(
+    adj_ref, own_ref, w1_ref, w2_ref, cot_hbm, agg2_ref, slope_ref, turned_ref, w1_out, w2_out, cot_ref, sem, *, groups
+):
+    copy = pltpu.make_async_copy(cot_hbm.at[0], cot_ref, sem)
+    copy.start()
     hidden = w2_ref.shape[0]
     depth = hidden // groups
     target = lax.broadcasted_iota(jnp.int32, (hidden, hidden), 0)
@@ -72,35 +85,42 @@
     value, slope = gelu_parts(dot(own_ref[...], w1))
     slope_ref[...] = slope
     agg2_ref[...] = dot(adj_ref[1], value.astype(jnp.bfloat16))
-
-
-def cross_kernel(adj_ref, cross_ref, w1_ref, near_ref, agg2_ref, slope_ref):
-    value, slope = gelu_parts(dot(cross_ref[...], w1_ref[...]))
+    nodes = own_ref.shape[0]
+    for part in range(3):
+        turned_ref[part * nodes : (part + 1) * nodes, :] = adj_ref[part].T
+    copy.wait()
+
+
+def other_kernel(adj_ref, other_ref, w1_ref, near_ref, agg2_ref, slope_ref):
+    value, slope = gelu_parts(dot(other_ref[...], w1_ref[...]))
     slope_ref[...] = slope
-    agg2_ref[...] = near_ref[...] + dot(adj_ref[0], value.astype(jnp.bfloat16))
+    agg2_ref[...] = near_ref[...] + dot(adj_ref[2], value.astype(jnp.bfloat16))
 
 
 def layers_kernel(
-    adj_ref, cross_ref, own_ref, other_ref, cot_ref, agg2_ref, own_slope_ref, cross_slope_ref, w1_ref, w2_ref, out_ref
+    adj_ref, cross_ref, own_ref, other_ref, cot_ref, agg2_ref, own_slope_ref, other_slope_ref, turned_ref,
+    w1_ref, w2_ref, out_ref,
 ):
-    value, slope = gelu_parts(dot(other_ref[...], w1_ref[...]))
-    agg2 = agg2_ref[...] + dot(adj_ref[2], value.astype(jnp.bfloat16))
+    nodes, features = own_ref.shape
+    cross = cross_ref[:nodes, :]
+    value, slope = gelu_parts(dot(cross, w1_ref[...]))
+    agg2 = agg2_ref[...] + dot(adj_ref[0], value.astype(jnp.bfloat16))
     agg2 = agg2.astype(jnp.bfloat16)
     unused, slope2 = gelu_parts(dot(agg2, w2_ref[...]))
-    dpre2 = (cot_ref[0].astype(jnp.float32) * slope2).astype(jnp.bfloat16)
+    dpre2 = (cot_ref[...].astype(jnp.float32) * slope2).astype(jnp.bfloat16)
     dagg2 = dot(dpre2, w2_ref[...], 1, 1).astype(jnp.bfloat16)
-    first = None
-    parts = ((cross_ref, cross_slope_ref[...]), (own_ref, own_slope_ref[...]), (other_ref, slope))
-    for part, (ref, slope) in enumerate(parts):
-        spread = dot(adj_ref[part], dagg2, 0, 0)
-        dpre1 = (spread * slope).astype(jnp.bfloat16)
-        term = dot(ref[...], dpre1, 0, 0)
-        first = term if first is None else first + term
-    second = dot(agg2, dpre2, 0, 0)
     groups, depth = out_ref.shape[0], out_ref.shape[1]
-    features = first.shape[0]
-    out_ref[:, :, :features] = first.T.astype(jnp.bfloat16).reshape(groups, depth, features)
+    second = dot(agg2.T, dpre2)
     out_ref[:, :, features:] = second.astype(jnp.bfloat16).reshape(groups, depth, second.shape[1])
+    spread = dot(turned_ref[...], dagg2)
+    slopes = (slope, own_slope_ref[...], other_slope_ref[...])
+    dpre1 = [
+        (spread[part * nodes : (part + 1) * nodes] * slope).astype(jnp.bfloat16)
+        for part, slope in enumerate(slopes)
+    ]
+    agg1 = jnp.concatenate([cross, own_ref[...], other_ref[...]], axis=0)
+    first = dot(agg1.T, jnp.concatenate(dpre1, axis=0)).astype(jnp.bfloat16).T
+    out_ref[:, :, :features] = first.reshape(groups, depth, features)
 
 
 def depth_sum_kernel(in_ref, first_ref, second_ref):
@@ -146,27 +166,39 @@
         compiler_params=pltpu.CompilerParams(vmem_limit_bytes=4 * MIB),
         name="adjacency",
     )(odd, tile_count, *[pltpu.with_memory_space_constraint(i, pltpu.HBM) for i in inputs])
-    agg1 = near + dot(adjacency[2], other) + dot(adjacency[0], cross)
-    agg1 = agg1.astype(jnp.bfloat16)
-
-    cross = cross_swap(agg1)
+    agg1, sent = pl.pallas_call(
+        aggregate_kernel,
+        out_shape=(
+            jax.ShapeDtypeStruct((nodes, in_features), jnp.bfloat16),
+            jax.ShapeDtypeStruct((nodes + 16, in_features), jnp.bfloat16),
+        ),
+        in_specs=[VMEM] * 4,
+        out_specs=(VMEM, VMEM),
+        compiler_params=pltpu.CompilerParams(vmem_limit_bytes=4 * MIB),
+        name="aggregate",
+    )(other, adjacency, near, cross)
+
+    cross = cross_swap(sent)
     other = core_swap(agg1)
-    agg2, own_slope, w_first, w_second = pl.pallas_call(
+    agg2, own_slope, turned, w_first, w_second, cotangent = pl.pallas_call(
         functools.partial(own_kernel, groups=plane),
         out_shape=(
             jax.ShapeDtypeStruct((nodes, hidden), jnp.float32),
             jax.ShapeDtypeStruct((nodes, hidden), jnp.float32),
+            jax.ShapeDtypeStruct((3 * nodes, nodes), jnp.bfloat16),
             jax.ShapeDtypeStruct(w_first.shape, w_first.dtype),
             jax.ShapeDtypeStruct(w_second.shape, w_second.dtype),
-        ),
-        in_specs=[VMEM] * 4,
-        out_specs=[VMEM] * 4,
+            jax.ShapeDtypeStruct((nodes, hidden), grad_out.dtype),
+        ),
+        in_specs=[VMEM] * 4 + [HBM],
+        out_specs=[VMEM] * 6,
+        scratch_shapes=[pltpu.SemaphoreType.DMA],
         compiler_params=pltpu.CompilerParams(vmem_limit_bytes=12 * MIB),
         cost_estimate=pl.CostEstimate(flops=600_000_000, bytes_accessed=4 * MIB, transcendentals=131072),
         name="own_part",
-    )(adjacency, agg1, w_first, w_second)
-    agg2, cross_slope = pl.pallas_call(
-        cross_kernel,
+    )(adjacency, agg1, w_first, w_second, pltpu.with_memory_space_constraint(grad_out, pltpu.HBM))
+    agg2, other_slope = pl.pallas_call(
+        other_kernel,
         out_shape=(
             jax.ShapeDtypeStruct((nodes, hidden), jnp.float32),
             jax.ShapeDtypeStruct((nodes, hidden), jnp.float32),
@@ -174,16 +206,16 @@
         in_specs=[VMEM] * 4,
         out_specs=[VMEM] * 2,
         compiler_params=pltpu.CompilerParams(vmem_limit_bytes=8 * MIB),
-        name="cross_part",
-    )(adjacency, cross, w_first, agg2)
+        name="other_part",
+    )(adjacency, other, w_first, agg2)
     gradients = pl.pallas_call(
         layers_kernel,
         out_shape=jax.ShapeDtypeStruct((plane, depth, in_features + hidden), jnp.bfloat16),
-        in_specs=[VMEM] * 10,
+        in_specs=[VMEM] * 11,
         out_specs=VMEM,
         compiler_params=pltpu.CompilerParams(vmem_limit_bytes=12 * MIB),
         name="layers",
-    )(adjacency, cross, agg1, other, grad_out, agg2, own_slope, cross_slope, w_first, w_second)
+    )(adjacency, cross, agg1, other, cotangent, agg2, own_slope, other_slope, turned, w_first, w_second)
 
     gathered = lax.all_to_all(gradients, PLANE, 0, 0, tiled=True)
     partial = jnp.sum(gathered.astype(jnp.float32), axis=0)

time: 67.9 us -> 66.9 us (0.985)
  transfers between devices with their start and end apart: 4 -> 4, of which waited for: 1 -> 0; matrix products, arithmetic and copies ran while one was open for 0% -> 0% of each run, Pallas kernels for 4% -> 5%
where the time goes in v4:
time: 66.9 us; the launch traced here: 66.6 us
  blocking collectives  46.1 us (69%)
  starting transfers between devices  13.4 us (20%)
  Pallas kernels  5.52 us (8%)
  between operations  1.41 us (2%)
    all_to_all x1, blocking collectives, body(): collected = lax.all_to_all(partial, 'z', 0, 0, tiled=True)  27.2 us
    all_to_all x1, blocking collectives, body(): gathered = lax.all_to_all(gradients, PLANE, 0, 0, tiled=True)  18.9 us
    ppermute x2, starting transfers between devices, core_swap(): return lax.ppermute(block, 'c', [(0, 1), (1, 0)])  6.78 us
    ppermute x2, starting transfers between devices, cross_swap(): return lax.ppermute(block, SECTION, pairs + [(j, i) for i, j in pairs])  6.65 us
    pallas_call x1, Pallas kernels, body(): pl.pallas_call(layers_kernel, out_shape=jax.ShapeDtypeStruct((plane, dept...  1.64 us
  transfers between devices with their start and end apart: 4, of which 0 were waited for; matrix products, arithmetic and copies ran while one was open for 0% of the time, Pallas kernels for 5%

profile of v4, /device:TPU:1, one launch (start us, length us, event | category | flops | bytes accessed | tf_op | source)
XLA Modules:
  0.0 66.6 jit_solution(17071123678336679720)
XLA Ops:
  0.6 0.0 copy-start
  0.6 0.0 copy-start.1
  0.7 4.7 %collective-permute-start.1 = (bf16[256,128]{1,0:T(8,128)(2,1)}, bf16[256,128]{1,0:T(8,128)(2,1)S(1)}, u32[]{:S(2)}, u32[]{:S(2)}) collective-permute-start(bf16[256,128]{1,0:T(8,128)(2,1)} %bitcast.2), channel_id=1, source_target_pairs={{4,8},{12,16},{20,24},{28,32},{36,40},{44,48},{52,56},{60,64},{68,... | collective-permute-start | bytes 196616 | tf_op jit(solution)/shard_map/ppermute | solution.py:137
  5.4 4.9 %collective-permute-start = (bf16[256,128]{1,0:T(8,128)(2,1)}, bf16[256,128]{1,0:T(8,128)(2,1)S(1)}, u32[]{:S(2)}, u32[]{:S(2)}) collective-permute-start(bf16[256,128]{1,0:T(8,128)(2,1)} %bitcast.3), channel_id=1, source_target_pairs={{0,4},{4,0},{1,5},{5,1},{2,6},{6,2},{3,7},{7,3},{8,12},{12,8},{9,1... | collective-permute-start | bytes 196616 | tf_op jit(solution)/shard_map/ppermute | solution.py:141
  10.9 1.3 %adjacency.1 = (bf16[3,256,256]{2,1,0:T(8,128)(2,1)S(1)}, f32[256,128]{1,0:T(8,128)S(1)}) custom-call(s32[1]{0:T(128)} %bitcast.odd_ref, s32[1,1]{1,0:T(1,128)S(6)} %copy.10.count_ref, s32[1,8]{1,0:T(1,128)} %rows_hbm.1, s32[1,8]{1,0:T(1,128)} %cols_hbm.1, bf16[1,8,128,128]{3,2,1,0:T(8,128)(2,1)} %tiles_hbm.1, bf16[1,256,128]{2,1,0:T(8,128)(2,1)} %own_hbm.1), custom_call_target="tpu_custom_call" | custom-call | tf_op jit(solution)/shard_map/adjacency/pallas_call | solution.py:155
  12.2 0.0 collective-permute-done.1.cross_ref
  12.2 0.0 collective-permute-done.other_ref
  12.2 0.2 aggregate.1
  12.4 1.9 %collective-permute-start.2 = (bf16[272,128]{1,0:T(8,128)(2,1)S(1)}, bf16[272,128]{1,0:T(8,128)(2,1)S(1)}, u32[]{:S(2)}, u32[]{:S(2)}) collective-permute-start(bf16[272,128]{1,0:T(8,128)(2,1)S(1)} %get-tuple-element.16), channel_id=1, source_target_pairs={{4,8},{12,16},{20,24},{28,32},{36,40},{44,48},{52,56},{60,64},{68,... | collective-permute-start | bytes 208904 | tf_op jit(solution)/shard_map/ppermute | solution.py:137
  14.4 1.9 %collective-permute-start.3 = (bf16[256,128]{1,0:T(8,128)(2,1)S(1)}, bf16[256,128]{1,0:T(8,128)(2,1)S(1)}, u32[]{:S(2)}, u32[]{:S(2)}) collective-permute-start(bf16[256,128]{1,0:T(8,128)(2,1)S(1)} %get-tuple-element.17.own_ref), channel_id=1, source_target_pairs={{0,4},{4,0},{1,5},{5,1},{2,6},{6,2},{3,7},{7,3},{8,12},{12,8},{9,1... | collective-permute-start | bytes 196616 | tf_op jit(solution)/shard_map/ppermute | solution.py:141
  16.3 0.0 copy-done
  16.3 0.0 copy-done.1
  16.3 1.2 %own_part.1 = (f32[256,512]{1,0:T(8,128)S(1)}, f32[256,512]{1,0:T(8,128)S(1)}, bf16[768,256]{1,0:T(8,128)(2,1)S(1)}, bf16[128,512]{1,0:T(8,128)(2,1)S(1)}, bf16[...) custom-call(bf16[3,256,256]{2,1,0:T(8,128)(2,1)S(1)} %get-tuple-element.14.adj_ref, ...), custom_call_target="tpu_custom_call" | custom-call | flops 600000000 | bytes 4194304 | tf_op jit(solution)/shard_map/own_part/pallas_call | solution.py:183
  17.5 0.0 collective-permute-done.3.other_ref
  17.5 0.6 other_part.1
  18.1 0.0 collective-permute-done.2.cross_ref
  18.2 1.6 %layers.1 = bf16[32,16,640]{2,1,0:T(8,128)(2,1)S(1)} custom-call(bf16[3,256,256]{2,1,0:T(8,128)(2,1)S(1)} %get-tuple-element.14.adj_ref, bf16[272,128]{1,0:T(8,128)(2,1)S(1)} %collective-permute-done.2.cross_ref, bf16[256,128]{1,0:T(8,128)(2,1)S(1)} %get-tuple-element.17.own_ref, bf16[256,128]{1,0:T(8,128)(2,1)S(1)} %collective-permute-done.3.other_ref, ...), custom_call_target="tpu_custom_call" | custom-call | tf_op jit(solution)/shard_map/layers/pallas_call | solution.py:211
  19.8 18.9 %all_to_all.10 = bf16[32,16,640]{2,1,0:T(8,128)(2,1)S(1)} all-to-all(bf16[32,16,640]{2,1,0:T(8,128)(2,1)S(1)} %layers.1), channel_id=1, replica_groups=mesh['z'=16,'y'=4,'c'=2,'x'=4] {'y','c','x'}, dimensions={0} | all-to-all | bytes 1310720 | tf_op jit(solution)/shard_map/all_to_all | solution.py:220
  38.7 0.1 convert_reduce_fusion
  38.8 27.2 %all_to_all.11.in_ref = f32[16,5,128]{2,1,0:T(8,128)S(1)} all-to-all(f32[16,5,128]{2,1,0:T(8,128)S(1)} %reshape.11), channel_id=1, replica_groups=mesh['z'=16,'y'=4,'c'=2,'x'=4] {'z'}, dimensions={0} | all-to-all | bytes 81920 | tf_op jit(solution)/shard_map/all_to_all | solution.py:223
  66.0 0.6 depth_sum.1
  (1 shorter events, 0.0 us)
Async XLA Ops:
  0.6 15.7 %copy-start = (bf16[512,512]{1,0:T(8,128)(2,1)S(1)}, bf16[512,512]{1,0:T(8,128)(2,1)}, u32[]{:S(2)}) copy-start(bf16[512,512]{1,0:T(8,128)(2,1)} %w2_ref.1) | copy-start | bytes 1572868
  0.6 15.7 %copy-start.1 = (bf16[128,512]{1,0:T(8,128)(2,1)S(1)}, bf16[128,512]{1,0:T(8,128)(2,1)}, u32[]{:S(2)}) copy-start(bf16[128,512]{1,0:T(8,128)(2,1)} %w1_ref.1) | copy-start | bytes 393220
  0.7 11.6 %collective-permute-start.1 = (bf16[256,128]{1,0:T(8,128)(2,1)}, bf16[256,128]{1,0:T(8,128)(2,1)S(1)}, u32[]{:S(2)}, u32[]{:S(2)}) collective-permute-start(bf16[256,128]{1,0:T(8,128)(2,1)} %bitcast.2), channel_id=1, source_target_pairs={{4,8},{12,16},{20,24},{28,32},{36,40},{44,48},{52,56},{60,64},{68,... | collective-permute-start | bytes 196616 | tf_op jit(solution)/shard_map/ppermute | solution.py:137
  5.4 6.8 %collective-permute-start = (bf16[256,128]{1,0:T(8,128)(2,1)}, bf16[256,128]{1,0:T(8,128)(2,1)S(1)}, u32[]{:S(2)}, u32[]{:S(2)}) collective-permute-start(bf16[256,128]{1,0:T(8,128)(2,1)} %bitcast.3), channel_id=1, source_target_pairs={{0,4},{4,0},{1,5},{5,1},{2,6},{6,2},{3,7},{7,3},{8,12},{12,8},{9,1... | collective-permute-start | bytes 196616 | tf_op jit(solution)/shard_map/ppermute | solution.py:141
  12.4 5.7 %collective-permute-start.2 = (bf16[272,128]{1,0:T(8,128)(2,1)S(1)}, bf16[272,128]{1,0:T(8,128)(2,1)S(1)}, u32[]{:S(2)}, u32[]{:S(2)}) collective-permute-start(bf16[272,128]{1,0:T(8,128)(2,1)S(1)} %get-tuple-element.16), channel_id=1, source_target_pairs={{4,8},{12,16},{20,24},{28,32},{36,40},{44,48},{52,56},{60,64},{68,... | collective-permute-start | bytes 208904 | tf_op jit(solution)/shard_map/ppermute | solution.py:137
  14.4 3.1 %collective-permute-start.3 = (bf16[256,128]{1,0:T(8,128)(2,1)S(1)}, bf16[256,128]{1,0:T(8,128)(2,1)S(1)}, u32[]{:S(2)}, u32[]{:S(2)}) collective-permute-start(bf16[256,128]{1,0:T(8,128)(2,1)S(1)} %get-tuple-element.17.own_ref), channel_id=1, source_target_pairs={{0,4},{4,0},{1,5},{5,1},{2,6},{6,2},{3,7},{7,3},{8,12},{12,8},{9,1... | collective-permute-start | bytes 196616 | tf_op jit(solution)/shard_map/ppermute | solution.py:141

commit v5 on v4

--- a/solution.py
+++ b/solution.py
@@ -14,6 +14,8 @@
 SCALE = 0.7978845608028654
 CUBIC = 0.044715
 MIB = 1024 * 1024
+DEPTH_FIRST = 8
+PLANE_FIRST = 30
 VMEM = pl.BlockSpec(memory_space=pltpu.VMEM)
 HBM = pl.BlockSpec(memory_space=pltpu.HBM)
 SMEM = pl.BlockSpec(memory_space=pltpu.SMEM)
@@ -78,7 +80,9 @@
     depth = hidden // groups
     target = lax.broadcasted_iota(jnp.int32, (hidden, hidden), 0)
     source = lax.broadcasted_iota(jnp.int32, (hidden, hidden), 1)
-    order = (source == (target % depth) * groups + target // depth).astype(jnp.bfloat16)
+    plane = (target % depth + DEPTH_FIRST) % depth
+    place = (target // depth + PLANE_FIRST) % groups
+    order = (source == plane * groups + place).astype(jnp.bfloat16)
     w1 = dot(w1_ref[...], order, 1, 1).astype(jnp.bfloat16)
     w1_out[...] = w1
     w2_out[...] = dot(order, w2_ref[...]).astype(jnp.bfloat16)
@@ -124,7 +128,7 @@
 
 
 def depth_sum_kernel(in_ref, first_ref, second_ref):
-    total = jnp.sum(in_ref[...], axis=0)
+    total = jnp.sum(in_ref[...].astype(jnp.float32), axis=0)
     pieces = first_ref.shape[1] // 128
     for piece in range(total.shape[0]):
         ref, place = (first_ref, piece) if piece < pieces else (second_ref, piece - pieces)
@@ -217,10 +221,12 @@
         name="layers",
     )(adjacency, cross, agg1, other, cotangent, agg2, own_slope, other_slope, turned, w_first, w_second)
 
-    gathered = lax.all_to_all(gradients, PLANE, 0, 0, tiled=True)
+    groups = [[(i + PLANE_FIRST) % plane for i in range(plane)]]
+    gathered = lax.all_to_all(gradients, PLANE, 0, 0, axis_index_groups=groups, tiled=True)
     partial = jnp.sum(gathered.astype(jnp.float32), axis=0)
-    partial = partial.reshape(depth, (in_features + hidden) // 128, 128)
-    collected = lax.all_to_all(partial, "z", 0, 0, tiled=True)
+    partial = partial.astype(jnp.bfloat16).reshape(depth, (in_features + hidden) // 128, 128)
+    groups = [[(i + DEPTH_FIRST) % depth for i in range(depth)]]
+    collected = lax.all_to_all(partial, "z", 0, 0, axis_index_groups=groups, tiled=True)
     return pl.pallas_call(
         depth_sum_kernel,
         out_shape=(

time: 66.9 us -> 59.3 us (0.89)
  blocking collectives: 46.1 us -> 38.4 us
    all_to_all x2, blocking collectives: 46.1 us -> 38.4 us  [the longest x1 21.6 us: body(): lax.all_to_all(partial, 'z', 0, 0, axis_index_groups=groups, tiled=True)]
where the time goes in v5:
time: 59.3 us; the launch traced here: 59 us
  blocking collectives  38.4 us (65%)
  starting transfers between devices  13.4 us (23%)
  Pallas kernels  5.6 us (9%)
  between operations  1.42 us (2%)
    all_to_all x1, blocking collectives, body(): lax.all_to_all(partial, 'z', 0, 0, axis_index_groups=groups, tiled=True)  21.6 us
    all_to_all x1, blocking collectives, body(): lax.all_to_all(gradients, PLANE, 0, 0, axis_index_groups=groups, tiled=True)  16.8 us
    ppermute x2, starting transfers between devices, core_swap(): return lax.ppermute(block, 'c', [(0, 1), (1, 0)])  6.78 us
    ppermute x2, starting transfers between devices, cross_swap(): return lax.ppermute(block, SECTION, pairs + [(j, i) for i, j in pairs])  6.65 us
    pallas_call x1, Pallas kernels, body(): pl.pallas_call(layers_kernel, out_shape=jax.ShapeDtypeStruct((plane, dept...  1.64 us
    pallas_call x1, Pallas kernels, body(): pl.pallas_call(adjacency_kernel, out_shape=(jax.ShapeDtypeStruct((3, node...  1.27 us
    pallas_call x1, Pallas kernels, body(): pl.pallas_call(functools.partial(own_kernel, groups=plane), out_shape=(ja...  1.25 us
  transfers between devices with their start and end apart: 4, of which 0 were waited for; matrix products, arithmetic and copies ran while one was open for 0% of the time, Pallas kernels for 5%

profile of v5, /device:TPU:1, one launch (start us, length us, event | category | flops | bytes accessed | tf_op | source)
XLA Modules:
  0.0 59.0 jit_solution(10151196538769885655)
XLA Ops:
  0.6 0.0 copy-start
  0.6 4.7 %collective-permute-start.1 = (bf16[256,128]{1,0:T(8,128)(2,1)}, bf16[256,128]{1,0:T(8,128)(2,1)S(1)}, u32[]{:S(2)}, u32[]{:S(2)}) collective-permute-start(bf16[256,128]{1,0:T(8,128)(2,1)} %bitcast.2), channel_id=1, source_target_pairs={{4,8},{12,16},{20,24},{28,32},{36,40},{44,48},{52,56},{60,64},{68,... | collective-permute-start | bytes 196616 | tf_op jit(solution)/shard_map/ppermute | solution.py:141
  5.4 4.9 %collective-permute-start = (bf16[256,128]{1,0:T(8,128)(2,1)}, bf16[256,128]{1,0:T(8,128)(2,1)S(1)}, u32[]{:S(2)}, u32[]{:S(2)}) collective-permute-start(bf16[256,128]{1,0:T(8,128)(2,1)} %bitcast.3), channel_id=1, source_target_pairs={{0,4},{4,0},{1,5},{5,1},{2,6},{6,2},{3,7},{7,3},{8,12},{12,8},{9,1... | collective-permute-start | bytes 196616 | tf_op jit(solution)/shard_map/ppermute | solution.py:145
  10.9 1.3 %adjacency.1 = (bf16[3,256,256]{2,1,0:T(8,128)(2,1)S(1)}, f32[256,128]{1,0:T(8,128)S(1)}) custom-call(s32[1]{0:T(128)} %bitcast.odd_ref, s32[1,1]{1,0:T(1,128)S(6)} %copy.10.count_ref, s32[1,8]{1,0:T(1,128)} %rows_hbm.1, s32[1,8]{1,0:T(1,128)} %cols_hbm.1, bf16[1,8,128,128]{3,2,1,0:T(8,128)(2,1)} %tiles_hbm.1, bf16[1,256,128]{2,1,0:T(8,128)(2,1)} %own_hbm.1), custom_call_target="tpu_custom_call" | custom-call | tf_op jit(solution)/shard_map/adjacency/pallas_call | solution.py:159
  12.2 0.0 collective-permute-done.1.cross_ref
  12.2 0.0 collective-permute-done.other_ref
  12.2 0.0 copy-start.1
  12.2 0.2 aggregate.1
  12.4 1.9 %collective-permute-start.2 = (bf16[272,128]{1,0:T(8,128)(2,1)S(1)}, bf16[272,128]{1,0:T(8,128)(2,1)S(1)}, u32[]{:S(2)}, u32[]{:S(2)}) collective-permute-start(bf16[272,128]{1,0:T(8,128)(2,1)S(1)} %get-tuple-element.16), channel_id=1, source_target_pairs={{4,8},{12,16},{20,24},{28,32},{36,40},{44,48},{52,56},{60,64},{68,... | collective-permute-start | bytes 208904 | tf_op jit(solution)/shard_map/ppermute | solution.py:141
  14.3 1.9 %collective-permute-start.3 = (bf16[256,128]{1,0:T(8,128)(2,1)S(1)}, bf16[256,128]{1,0:T(8,128)(2,1)S(1)}, u32[]{:S(2)}, u32[]{:S(2)}) collective-permute-start(bf16[256,128]{1,0:T(8,128)(2,1)S(1)} %get-tuple-element.17.own_ref), channel_id=1, source_target_pairs={{0,4},{4,0},{1,5},{5,1},{2,6},{6,2},{3,7},{7,3},{8,12},{12,8},{9,1... | collective-permute-start | bytes 196616 | tf_op jit(solution)/shard_map/ppermute | solution.py:145
  16.3 0.0 copy-done
  16.3 0.0 copy-done.1
  16.3 1.2 %own_part.1 = (f32[256,512]{1,0:T(8,128)S(1)}, f32[256,512]{1,0:T(8,128)S(1)}, bf16[768,256]{1,0:T(8,128)(2,1)S(1)}, bf16[128,512]{1,0:T(8,128)(2,1)S(1)}, bf16[...) custom-call(bf16[3,256,256]{2,1,0:T(8,128)(2,1)S(1)} %get-tuple-element.14.adj_ref, ...), custom_call_target="tpu_custom_call" | custom-call | flops 600000000 | bytes 4194304 | tf_op jit(solution)/shard_map/own_part/pallas_call | solution.py:187
  17.5 0.0 collective-permute-done.3.other_ref
  17.6 0.6 %other_part.1 = (f32[256,512]{1,0:T(8,128)S(1)}, f32[256,512]{1,0:T(8,128)S(1)}) custom-call(bf16[3,256,256]{2,1,0:T(8,128)(2,1)S(1)} %get-tuple-element.14.adj_ref, bf16[256,128]{1,0:T(8,128)(2,1)S(1)} %collective-permute-done.3.other_ref, bf16[128,512]{1,0:T(8,128)(2,1)S(1)} %get-tuple-element.19.w1_ref, f32[256,512]{1,0:T(8,128)S(1)} %get-tuple-element.20.near_ref), custom_call_target="tpu_custom_call" | custom-call | tf_op jit(solution)/shard_map/other_part/pallas_call | solution.py:204
  18.2 0.0 collective-permute-done.2.cross_ref
  18.2 1.6 %layers.1 = bf16[32,16,640]{2,1,0:T(8,128)(2,1)S(1)} custom-call(bf16[3,256,256]{2,1,0:T(8,128)(2,1)S(1)} %get-tuple-element.14.adj_ref, bf16[272,128]{1,0:T(8,128)(2,1)S(1)} %collective-permute-done.2.cross_ref, bf16[256,128]{1,0:T(8,128)(2,1)S(1)} %get-tuple-element.17.own_ref, bf16[256,128]{1,0:T(8,128)(2,1)S(1)} %collective-permute-done.3.other_ref, ...), custom_call_target="tpu_custom_call" | custom-call | tf_op jit(solution)/shard_map/layers/pallas_call | solution.py:215
  19.9 16.8 %all_to_all.10 = bf16[32,16,640]{2,1,0:T(8,128)(2,1)S(1)} all-to-all(bf16[32,16,640]{2,1,0:T(8,128)(2,1)S(1)} %layers.1), channel_id=1, replica_groups={{30,31,0,1,2,3,4,5,6,7,8,9,10,11,12,13,14,15,16,17,18,19,20,21,22,23,24..., dimensions={0} | all-to-all | bytes 1310720 | tf_op jit(solution)/shard_map/all_to_all | solution.py:225
  36.6 0.1 reduce_sum.12
  36.8 21.6 %all_to_all.11.in_ref = bf16[16,5,128]{2,1,0:T(8,128)(2,1)S(1)} all-to-all(bf16[16,5,128]{2,1,0:T(8,128)(2,1)S(1)} %reshape.11), channel_id=1, replica_groups={{256,288,320,352,384,416,448,480,0,32,64,96,128,160,192,224},{257,289,3..., dimensions={0} | all-to-all | bytes 40960 | tf_op jit(solution)/shard_map/all_to_all | solution.py:229
  58.4 0.6 %depth_sum.1 = (f32[1,128]{1,0:T(1,128)}, f32[1,512]{1,0:T(1,128)}) custom-call(bf16[16,5,128]{2,1,0:T(8,128)(2,1)S(1)} %all_to_all.11.in_ref), custom_call_target="tpu_custom_call" | custom-call | tf_op jit(solution)/shard_map/depth_sum/pallas_call | solution.py:230
  (1 shorter events, 0.0 us)
Async XLA Ops:
  0.6 15.6 %copy-start = (bf16[512,512]{1,0:T(8,128)(2,1)S(1)}, bf16[512,512]{1,0:T(8,128)(2,1)}, u32[]{:S(2)}) copy-start(bf16[512,512]{1,0:T(8,128)(2,1)} %w2_ref.1) | copy-start | bytes 1572868
  0.6 11.5 %collective-permute-start.1 = (bf16[256,128]{1,0:T(8,128)(2,1)}, bf16[256,128]{1,0:T(8,128)(2,1)S(1)}, u32[]{:S(2)}, u32[]{:S(2)}) collective-permute-start(bf16[256,128]{1,0:T(8,128)(2,1)} %bitcast.2), channel_id=1, source_target_pairs={{4,8},{12,16},{20,24},{28,32},{36,40},{44,48},{52,56},{60,64},{68,... | collective-permute-start | bytes 196616 | tf_op jit(solution)/shard_map/ppermute | solution.py:141
  5.4 6.8 %collective-permute-start = (bf16[256,128]{1,0:T(8,128)(2,1)}, bf16[256,128]{1,0:T(8,128)(2,1)S(1)}, u32[]{:S(2)}, u32[]{:S(2)}) collective-permute-start(bf16[256,128]{1,0:T(8,128)(2,1)} %bitcast.3), channel_id=1, source_target_pairs={{0,4},{4,0},{1,5},{5,1},{2,6},{6,2},{3,7},{7,3},{8,12},{12,8},{9,1... | collective-permute-start | bytes 196616 | tf_op jit(solution)/shard_map/ppermute | solution.py:145
  12.2 4.1 %copy-start.1 = (bf16[128,512]{1,0:T(8,128)(2,1)S(1)}, bf16[128,512]{1,0:T(8,128)(2,1)}, u32[]{:S(2)}) copy-start(bf16[128,512]{1,0:T(8,128)(2,1)} %w1_ref.1) | copy-start | bytes 393220
  12.4 5.8 %collective-permute-start.2 = (bf16[272,128]{1,0:T(8,128)(2,1)S(1)}, bf16[272,128]{1,0:T(8,128)(2,1)S(1)}, u32[]{:S(2)}, u32[]{:S(2)}) collective-permute-start(bf16[272,128]{1,0:T(8,128)(2,1)S(1)} %get-tuple-element.16), channel_id=1, source_target_pairs={{4,8},{12,16},{20,24},{28,32},{36,40},{44,48},{52,56},{60,64},{68,... | collective-permute-start | bytes 208904 | tf_op jit(solution)/shard_map/ppermute | solution.py:141
  14.3 3.2 %collective-permute-start.3 = (bf16[256,128]{1,0:T(8,128)(2,1)S(1)}, bf16[256,128]{1,0:T(8,128)(2,1)S(1)}, u32[]{:S(2)}, u32[]{:S(2)}) collective-permute-start(bf16[256,128]{1,0:T(8,128)(2,1)S(1)} %get-tuple-element.17.own_ref), channel_id=1, source_target_pairs={{0,4},{4,0},{1,5},{5,1},{2,6},{6,2},{3,7},{7,3},{8,12},{12,8},{9,1... | collective-permute-start | bytes 196616 | tf_op jit(solution)/shard_map/ppermute | solution.py:145

commit v6 on v5

--- a/solution.py
+++ b/solution.py
@@ -14,8 +14,8 @@
 SCALE = 0.7978845608028654
 CUBIC = 0.044715
 MIB = 1024 * 1024
-DEPTH_FIRST = 8
-PLANE_FIRST = 30
+DEPTH_FIRST = 9
+PLANE_FIRST = 22
 VMEM = pl.BlockSpec(memory_space=pltpu.VMEM)
 HBM = pl.BlockSpec(memory_space=pltpu.HBM)
 SMEM = pl.BlockSpec(memory_space=pltpu.SMEM)

time: 59.3 us -> 59 us (level)
    all_to_all x1, blocking collectives: 16.8 us -> 16.1 us  [body(): lax.all_to_all(gradients, PLANE, 0, 0, axis_index_groups=groups, tiled=True)]
where the time goes in v6:
time: 59 us; the launch traced here: 58.6 us
  blocking collectives  38 us (64%)
  starting transfers between devices  13.4 us (23%)
  Pallas kernels  5.59 us (9%)
  between operations  1.42 us (2%)
    all_to_all x1, blocking collectives, body(): lax.all_to_all(partial, 'z', 0, 0, axis_index_groups=groups, tiled=True)  21.9 us
    all_to_all x1, blocking collectives, body(): lax.all_to_all(gradients, PLANE, 0, 0, axis_index_groups=groups, tiled=True)  16.1 us
    ppermute x2, starting transfers between devices, core_swap(): return lax.ppermute(block, 'c', [(0, 1), (1, 0)])  6.78 us
    ppermute x2, starting transfers between devices, cross_swap(): return lax.ppermute(block, SECTION, pairs + [(j, i) for i, j in pairs])  6.65 us
    pallas_call x1, Pallas kernels, body(): pl.pallas_call(layers_kernel, out_shape=jax.ShapeDtypeStruct((plane, dept...  1.64 us
    pallas_call x1, Pallas kernels, body(): pl.pallas_call(adjacency_kernel, out_shape=(jax.ShapeDtypeStruct((3, node...  1.26 us
    pallas_call x1, Pallas kernels, body(): pl.pallas_call(functools.partial(own_kernel, groups=plane), out_shape=(ja...  1.25 us
  transfers between devices with their start and end apart: 4, of which 0 were waited for; matrix products, arithmetic and copies ran while one was open for 0% of the time, Pallas kernels for 5%

profile of v6, /device:TPU:1, one launch (start us, length us, event | category | flops | bytes accessed | tf_op | source)
XLA Modules:
  0.0 58.6 jit_solution(11852942196416858121)
XLA Ops:
  0.6 0.0 copy-start
  0.6 4.7 %collective-permute-start.1 = (bf16[256,128]{1,0:T(8,128)(2,1)}, bf16[256,128]{1,0:T(8,128)(2,1)S(1)}, u32[]{:S(2)}, u32[]{:S(2)}) collective-permute-start(bf16[256,128]{1,0:T(8,128)(2,1)} %bitcast.2), channel_id=1, source_target_pairs={{4,8},{12,16},{20,24},{28,32},{36,40},{44,48},{52,56},{60,64},{68,... | collective-permute-start | bytes 196616 | tf_op jit(solution)/shard_map/ppermute | solution.py:141
  5.4 4.9 %collective-permute-start = (bf16[256,128]{1,0:T(8,128)(2,1)}, bf16[256,128]{1,0:T(8,128)(2,1)S(1)}, u32[]{:S(2)}, u32[]{:S(2)}) collective-permute-start(bf16[256,128]{1,0:T(8,128)(2,1)} %bitcast.3), channel_id=1, source_target_pairs={{0,4},{4,0},{1,5},{5,1},{2,6},{6,2},{3,7},{7,3},{8,12},{12,8},{9,1... | collective-permute-start | bytes 196616 | tf_op jit(solution)/shard_map/ppermute | solution.py:145
  10.9 1.3 %adjacency.1 = (bf16[3,256,256]{2,1,0:T(8,128)(2,1)S(1)}, f32[256,128]{1,0:T(8,128)S(1)}) custom-call(s32[1]{0:T(128)} %bitcast.odd_ref, s32[1,1]{1,0:T(1,128)S(6)} %copy.10.count_ref, s32[1,8]{1,0:T(1,128)} %rows_hbm.1, s32[1,8]{1,0:T(1,128)} %cols_hbm.1, bf16[1,8,128,128]{3,2,1,0:T(8,128)(2,1)} %tiles_hbm.1, bf16[1,256,128]{2,1,0:T(8,128)(2,1)} %own_hbm.1), custom_call_target="tpu_custom_call" | custom-call | tf_op jit(solution)/shard_map/adjacency/pallas_call | solution.py:159
  12.2 0.0 collective-permute-done.1.cross_ref
  12.2 0.0 collective-permute-done.other_ref
  12.2 0.0 copy-start.1
  12.2 0.2 aggregate.1
  12.4 1.9 %collective-permute-start.2 = (bf16[272,128]{1,0:T(8,128)(2,1)S(1)}, bf16[272,128]{1,0:T(8,128)(2,1)S(1)}, u32[]{:S(2)}, u32[]{:S(2)}) collective-permute-start(bf16[272,128]{1,0:T(8,128)(2,1)S(1)} %get-tuple-element.16), channel_id=1, source_target_pairs={{4,8},{12,16},{20,24},{28,32},{36,40},{44,48},{52,56},{60,64},{68,... | collective-permute-start | bytes 208904 | tf_op jit(solution)/shard_map/ppermute | solution.py:141
  14.3 1.9 %collective-permute-start.3 = (bf16[256,128]{1,0:T(8,128)(2,1)S(1)}, bf16[256,128]{1,0:T(8,128)(2,1)S(1)}, u32[]{:S(2)}, u32[]{:S(2)}) collective-permute-start(bf16[256,128]{1,0:T(8,128)(2,1)S(1)} %get-tuple-element.17.own_ref), channel_id=1, source_target_pairs={{0,4},{4,0},{1,5},{5,1},{2,6},{6,2},{3,7},{7,3},{8,12},{12,8},{9,1... | collective-permute-start | bytes 196616 | tf_op jit(solution)/shard_map/ppermute | solution.py:145
  16.3 0.0 copy-done
  16.3 0.0 copy-done.1
  16.3 1.3 %own_part.1 = (f32[256,512]{1,0:T(8,128)S(1)}, f32[256,512]{1,0:T(8,128)S(1)}, bf16[768,256]{1,0:T(8,128)(2,1)S(1)}, bf16[128,512]{1,0:T(8,128)(2,1)S(1)}, bf16[...) custom-call(bf16[3,256,256]{2,1,0:T(8,128)(2,1)S(1)} %get-tuple-element.14.adj_ref, ...), custom_call_target="tpu_custom_call" | custom-call | flops 600000000 | bytes 4194304 | tf_op jit(solution)/shard_map/own_part/pallas_call | solution.py:187
  17.5 0.0 collective-permute-done.3.other_ref
  17.6 0.6 %other_part.1 = (f32[256,512]{1,0:T(8,128)S(1)}, f32[256,512]{1,0:T(8,128)S(1)}) custom-call(bf16[3,256,256]{2,1,0:T(8,128)(2,1)S(1)} %get-tuple-element.14.adj_ref, bf16[256,128]{1,0:T(8,128)(2,1)S(1)} %collective-permute-done.3.other_ref, bf16[128,512]{1,0:T(8,128)(2,1)S(1)} %get-tuple-element.19.w1_ref, f32[256,512]{1,0:T(8,128)S(1)} %get-tuple-element.20.near_ref), custom_call_target="tpu_custom_call" | custom-call | tf_op jit(solution)/shard_map/other_part/pallas_call | solution.py:204
  18.2 0.0 collective-permute-done.2.cross_ref
  18.2 1.6 %layers.1 = bf16[32,16,640]{2,1,0:T(8,128)(2,1)S(1)} custom-call(bf16[3,256,256]{2,1,0:T(8,128)(2,1)S(1)} %get-tuple-element.14.adj_ref, bf16[272,128]{1,0:T(8,128)(2,1)S(1)} %collective-permute-done.2.cross_ref, bf16[256,128]{1,0:T(8,128)(2,1)S(1)} %get-tuple-element.17.own_ref, bf16[256,128]{1,0:T(8,128)(2,1)S(1)} %collective-permute-done.3.other_ref, ...), custom_call_target="tpu_custom_call" | custom-call | tf_op jit(solution)/shard_map/layers/pallas_call | solution.py:215
  19.8 16.1 %all_to_all.10 = bf16[32,16,640]{2,1,0:T(8,128)(2,1)S(1)} all-to-all(bf16[32,16,640]{2,1,0:T(8,128)(2,1)S(1)} %layers.1), channel_id=1, replica_groups={{22,23,24,25,26,27,28,29,30,31,0,1,2,3,4,5,6,7,8,9,10,11,12,13,14,15,16..., dimensions={0} | all-to-all | bytes 1310720 | tf_op jit(solution)/shard_map/all_to_all | solution.py:225
  35.9 0.1 reduce_sum.12
  36.1 21.9 %all_to_all.11.in_ref = bf16[16,5,128]{2,1,0:T(8,128)(2,1)S(1)} all-to-all(bf16[16,5,128]{2,1,0:T(8,128)(2,1)S(1)} %reshape.11), channel_id=1, replica_groups={{288,320,352,384,416,448,480,0,32,64,96,128,160,192,224,256},{289,321,3..., dimensions={0} | all-to-all | bytes 40960 | tf_op jit(solution)/shard_map/all_to_all | solution.py:229
  58.0 0.6 %depth_sum.1 = (f32[1,128]{1,0:T(1,128)}, f32[1,512]{1,0:T(1,128)}) custom-call(bf16[16,5,128]{2,1,0:T(8,128)(2,1)S(1)} %all_to_all.11.in_ref), custom_call_target="tpu_custom_call" | custom-call | tf_op jit(solution)/shard_map/depth_sum/pallas_call | solution.py:230
  (1 shorter events, 0.0 us)
Async XLA Ops:
  0.6 15.6 %copy-start = (bf16[512,512]{1,0:T(8,128)(2,1)S(1)}, bf16[512,512]{1,0:T(8,128)(2,1)}, u32[]{:S(2)}) copy-start(bf16[512,512]{1,0:T(8,128)(2,1)} %w2_ref.1) | copy-start | bytes 1572868
  0.6 11.5 %collective-permute-start.1 = (bf16[256,128]{1,0:T(8,128)(2,1)}, bf16[256,128]{1,0:T(8,128)(2,1)S(1)}, u32[]{:S(2)}, u32[]{:S(2)}) collective-permute-start(bf16[256,128]{1,0:T(8,128)(2,1)} %bitcast.2), channel_id=1, source_target_pairs={{4,8},{12,16},{20,24},{28,32},{36,40},{44,48},{52,56},{60,64},{68,... | collective-permute-start | bytes 196616 | tf_op jit(solution)/shard_map/ppermute | solution.py:141
  5.4 6.8 %collective-permute-start = (bf16[256,128]{1,0:T(8,128)(2,1)}, bf16[256,128]{1,0:T(8,128)(2,1)S(1)}, u32[]{:S(2)}, u32[]{:S(2)}) collective-permute-start(bf16[256,128]{1,0:T(8,128)(2,1)} %bitcast.3), channel_id=1, source_target_pairs={{0,4},{4,0},{1,5},{5,1},{2,6},{6,2},{3,7},{7,3},{8,12},{12,8},{9,1... | collective-permute-start | bytes 196616 | tf_op jit(solution)/shard_map/ppermute | solution.py:145
  12.2 4.1 %copy-start.1 = (bf16[128,512]{1,0:T(8,128)(2,1)S(1)}, bf16[128,512]{1,0:T(8,128)(2,1)}, u32[]{:S(2)}) copy-start(bf16[128,512]{1,0:T(8,128)(2,1)} %w1_ref.1) | copy-start | bytes 393220
  12.4 5.8 %collective-permute-start.2 = (bf16[272,128]{1,0:T(8,128)(2,1)S(1)}, bf16[272,128]{1,0:T(8,128)(2,1)S(1)}, u32[]{:S(2)}, u32[]{:S(2)}) collective-permute-start(bf16[272,128]{1,0:T(8,128)(2,1)S(1)} %get-tuple-element.16), channel_id=1, source_target_pairs={{4,8},{12,16},{20,24},{28,32},{36,40},{44,48},{52,56},{60,64},{68,... | collective-permute-start | bytes 208904 | tf_op jit(solution)/shard_map/ppermute | solution.py:141
  14.3 3.2 %collective-permute-start.3 = (bf16[256,128]{1,0:T(8,128)(2,1)S(1)}, bf16[256,128]{1,0:T(8,128)(2,1)S(1)}, u32[]{:S(2)}, u32[]{:S(2)}) collective-permute-start(bf16[256,128]{1,0:T(8,128)(2,1)S(1)} %get-tuple-element.17.own_ref), channel_id=1, source_target_pairs={{0,4},{4,0},{1,5},{5,1},{2,6},{6,2},{3,7},{7,3},{8,12},{12,8},{9,1... | collective-permute-start | bytes 196616 | tf_op jit(solution)/shard_map/ppermute | solution.py:145

commit v7 on v6

--- a/solution.py
+++ b/solution.py
@@ -14,7 +14,7 @@
 SCALE = 0.7978845608028654
 CUBIC = 0.044715
 MIB = 1024 * 1024
-DEPTH_FIRST = 9
+DEPTH_FIRST = 10
 PLANE_FIRST = 22
 VMEM = pl.BlockSpec(memory_space=pltpu.VMEM)
 HBM = pl.BlockSpec(memory_space=pltpu.HBM)

time: 59 us -> 59 us (level)
  no operation moved by 1% of the time
where the time goes in v7:
time: 59 us; the launch traced here: 58.6 us
  blocking collectives  38 us (64%)
  starting transfers between devices  13.4 us (23%)
  Pallas kernels  5.6 us (9%)
  between operations  1.42 us (2%)
    all_to_all x1, blocking collectives, body(): lax.all_to_all(partial, 'z', 0, 0, axis_index_groups=groups, tiled=True)  21.9 us
    all_to_all x1, blocking collectives, body(): lax.all_to_all(gradients, PLANE, 0, 0, axis_index_groups=groups, tiled=True)  16 us
    ppermute x2, starting transfers between devices, core_swap(): return lax.ppermute(block, 'c', [(0, 1), (1, 0)])  6.78 us
    ppermute x2, starting transfers between devices, cross_swap(): return lax.ppermute(block, SECTION, pairs + [(j, i) for i, j in pairs])  6.65 us
    pallas_call x1, Pallas kernels, body(): pl.pallas_call(layers_kernel, out_shape=jax.ShapeDtypeStruct((plane, dept...  1.64 us
    pallas_call x1, Pallas kernels, body(): pl.pallas_call(adjacency_kernel, out_shape=(jax.ShapeDtypeStruct((3, node...  1.27 us
    pallas_call x1, Pallas kernels, body(): pl.pallas_call(functools.partial(own_kernel, groups=plane), out_shape=(ja...  1.25 us
  transfers between devices with their start and end apart: 4, of which 0 were waited for; matrix products, arithmetic and copies ran while one was open for 0% of the time, Pallas kernels for 5%

profile of v7, /device:TPU:1, one launch (start us, length us, event | category | flops | bytes accessed | tf_op | source)
XLA Modules:
  0.0 58.6 jit_solution(9433390822550172235)
XLA Ops:
  0.6 0.0 copy-start
  0.6 4.7 %collective-permute-start.1 = (bf16[256,128]{1,0:T(8,128)(2,1)}, bf16[256,128]{1,0:T(8,128)(2,1)S(1)}, u32[]{:S(2)}, u32[]{:S(2)}) collective-permute-start(bf16[256,128]{1,0:T(8,128)(2,1)} %bitcast.2), channel_id=1, source_target_pairs={{4,8},{12,16},{20,24},{28,32},{36,40},{44,48},{52,56},{60,64},{68,... | collective-permute-start | bytes 196616 | tf_op jit(solution)/shard_map/ppermute | solution.py:141
  5.4 4.9 %collective-permute-start = (bf16[256,128]{1,0:T(8,128)(2,1)}, bf16[256,128]{1,0:T(8,128)(2,1)S(1)}, u32[]{:S(2)}, u32[]{:S(2)}) collective-permute-start(bf16[256,128]{1,0:T(8,128)(2,1)} %bitcast.3), channel_id=1, source_target_pairs={{0,4},{4,0},{1,5},{5,1},{2,6},{6,2},{3,7},{7,3},{8,12},{12,8},{9,1... | collective-permute-start | bytes 196616 | tf_op jit(solution)/shard_map/ppermute | solution.py:145
  10.9 1.3 %adjacency.1 = (bf16[3,256,256]{2,1,0:T(8,128)(2,1)S(1)}, f32[256,128]{1,0:T(8,128)S(1)}) custom-call(s32[1]{0:T(128)} %bitcast.odd_ref, s32[1,1]{1,0:T(1,128)S(6)} %copy.10.count_ref, s32[1,8]{1,0:T(1,128)} %rows_hbm.1, s32[1,8]{1,0:T(1,128)} %cols_hbm.1, bf16[1,8,128,128]{3,2,1,0:T(8,128)(2,1)} %tiles_hbm.1, bf16[1,256,128]{2,1,0:T(8,128)(2,1)} %own_hbm.1), custom_call_target="tpu_custom_call" | custom-call | tf_op jit(solution)/shard_map/adjacency/pallas_call | solution.py:159
  12.2 0.0 collective-permute-done.1.cross_ref
  12.2 0.0 collective-permute-done.other_ref
  12.2 0.0 copy-start.1
  12.2 0.2 aggregate.1
  12.4 1.9 %collective-permute-start.2 = (bf16[272,128]{1,0:T(8,128)(2,1)S(1)}, bf16[272,128]{1,0:T(8,128)(2,1)S(1)}, u32[]{:S(2)}, u32[]{:S(2)}) collective-permute-start(bf16[272,128]{1,0:T(8,128)(2,1)S(1)} %get-tuple-element.16), channel_id=1, source_target_pairs={{4,8},{12,16},{20,24},{28,32},{36,40},{44,48},{52,56},{60,64},{68,... | collective-permute-start | bytes 208904 | tf_op jit(solution)/shard_map/ppermute | solution.py:141
  14.3 1.9 %collective-permute-start.3 = (bf16[256,128]{1,0:T(8,128)(2,1)S(1)}, bf16[256,128]{1,0:T(8,128)(2,1)S(1)}, u32[]{:S(2)}, u32[]{:S(2)}) collective-permute-start(bf16[256,128]{1,0:T(8,128)(2,1)S(1)} %get-tuple-element.17.own_ref), channel_id=1, source_target_pairs={{0,4},{4,0},{1,5},{5,1},{2,6},{6,2},{3,7},{7,3},{8,12},{12,8},{9,1... | collective-permute-start | bytes 196616 | tf_op jit(solution)/shard_map/ppermute | solution.py:145
  16.3 0.0 copy-done
  16.3 0.0 copy-done.1
  16.3 1.2 %own_part.1 = (f32[256,512]{1,0:T(8,128)S(1)}, f32[256,512]{1,0:T(8,128)S(1)}, bf16[768,256]{1,0:T(8,128)(2,1)S(1)}, bf16[128,512]{1,0:T(8,128)(2,1)S(1)}, bf16[...) custom-call(bf16[3,256,256]{2,1,0:T(8,128)(2,1)S(1)} %get-tuple-element.14.adj_ref, ...), custom_call_target="tpu_custom_call" | custom-call | flops 600000000 | bytes 4194304 | tf_op jit(solution)/shard_map/own_part/pallas_call | solution.py:187
  17.5 0.0 collective-permute-done.3.other_ref
  17.6 0.6 %other_part.1 = (f32[256,512]{1,0:T(8,128)S(1)}, f32[256,512]{1,0:T(8,128)S(1)}) custom-call(bf16[3,256,256]{2,1,0:T(8,128)(2,1)S(1)} %get-tuple-element.14.adj_ref, bf16[256,128]{1,0:T(8,128)(2,1)S(1)} %collective-permute-done.3.other_ref, bf16[128,512]{1,0:T(8,128)(2,1)S(1)} %get-tuple-element.19.w1_ref, f32[256,512]{1,0:T(8,128)S(1)} %get-tuple-element.20.near_ref), custom_call_target="tpu_custom_call" | custom-call | tf_op jit(solution)/shard_map/other_part/pallas_call | solution.py:204
  18.2 0.0 collective-permute-done.2.cross_ref
  18.2 1.6 %layers.1 = bf16[32,16,640]{2,1,0:T(8,128)(2,1)S(1)} custom-call(bf16[3,256,256]{2,1,0:T(8,128)(2,1)S(1)} %get-tuple-element.14.adj_ref, bf16[272,128]{1,0:T(8,128)(2,1)S(1)} %collective-permute-done.2.cross_ref, bf16[256,128]{1,0:T(8,128)(2,1)S(1)} %get-tuple-element.17.own_ref, bf16[256,128]{1,0:T(8,128)(2,1)S(1)} %collective-permute-done.3.other_ref, ...), custom_call_target="tpu_custom_call" | custom-call | tf_op jit(solution)/shard_map/layers/pallas_call | solution.py:215
  19.9 16.0 %all_to_all.10 = bf16[32,16,640]{2,1,0:T(8,128)(2,1)S(1)} all-to-all(bf16[32,16,640]{2,1,0:T(8,128)(2,1)S(1)} %layers.1), channel_id=1, replica_groups={{22,23,24,25,26,27,28,29,30,31,0,1,2,3,4,5,6,7,8,9,10,11,12,13,14,15,16..., dimensions={0} | all-to-all | bytes 1310720 | tf_op jit(solution)/shard_map/all_to_all | solution.py:225
  35.9 0.1 reduce_sum.12
  36.1 21.9 %all_to_all.11.in_ref = bf16[16,5,128]{2,1,0:T(8,128)(2,1)S(1)} all-to-all(bf16[16,5,128]{2,1,0:T(8,128)(2,1)S(1)} %reshape.11), channel_id=1, replica_groups={{320,352,384,416,448,480,0,32,64,96,128,160,192,224,256,288},{321,353,3..., dimensions={0} | all-to-all | bytes 40960 | tf_op jit(solution)/shard_map/all_to_all | solution.py:229
  58.0 0.6 %depth_sum.1 = (f32[1,128]{1,0:T(1,128)}, f32[1,512]{1,0:T(1,128)}) custom-call(bf16[16,5,128]{2,1,0:T(8,128)(2,1)S(1)} %all_to_all.11.in_ref), custom_call_target="tpu_custom_call" | custom-call | tf_op jit(solution)/shard_map/depth_sum/pallas_call | solution.py:230
  (1 shorter events, 0.0 us)
Async XLA Ops:
  0.6 15.6 %copy-start = (bf16[512,512]{1,0:T(8,128)(2,1)S(1)}, bf16[512,512]{1,0:T(8,128)(2,1)}, u32[]{:S(2)}) copy-start(bf16[512,512]{1,0:T(8,128)(2,1)} %w2_ref.1) | copy-start | bytes 1572868
  0.6 11.5 %collective-permute-start.1 = (bf16[256,128]{1,0:T(8,128)(2,1)}, bf16[256,128]{1,0:T(8,128)(2,1)S(1)}, u32[]{:S(2)}, u32[]{:S(2)}) collective-permute-start(bf16[256,128]{1,0:T(8,128)(2,1)} %bitcast.2), channel_id=1, source_target_pairs={{4,8},{12,16},{20,24},{28,32},{36,40},{44,48},{52,56},{60,64},{68,... | collective-permute-start | bytes 196616 | tf_op jit(solution)/shard_map/ppermute | solution.py:141
  5.4 6.8 %collective-permute-start = (bf16[256,128]{1,0:T(8,128)(2,1)}, bf16[256,128]{1,0:T(8,128)(2,1)S(1)}, u32[]{:S(2)}, u32[]{:S(2)}) collective-permute-start(bf16[256,128]{1,0:T(8,128)(2,1)} %bitcast.3), channel_id=1, source_target_pairs={{0,4},{4,0},{1,5},{5,1},{2,6},{6,2},{3,7},{7,3},{8,12},{12,8},{9,1... | collective-permute-start | bytes 196616 | tf_op jit(solution)/shard_map/ppermute | solution.py:145
  12.2 4.1 %copy-start.1 = (bf16[128,512]{1,0:T(8,128)(2,1)S(1)}, bf16[128,512]{1,0:T(8,128)(2,1)}, u32[]{:S(2)}) copy-start(bf16[128,512]{1,0:T(8,128)(2,1)} %w1_ref.1) | copy-start | bytes 393220
  12.4 5.8 %collective-permute-start.2 = (bf16[272,128]{1,0:T(8,128)(2,1)S(1)}, bf16[272,128]{1,0:T(8,128)(2,1)S(1)}, u32[]{:S(2)}, u32[]{:S(2)}) collective-permute-start(bf16[272,128]{1,0:T(8,128)(2,1)S(1)} %get-tuple-element.16), channel_id=1, source_target_pairs={{4,8},{12,16},{20,24},{28,32},{36,40},{44,48},{52,56},{60,64},{68,... | collective-permute-start | bytes 208904 | tf_op jit(solution)/shard_map/ppermute | solution.py:141
  14.3 3.2 %collective-permute-start.3 = (bf16[256,128]{1,0:T(8,128)(2,1)S(1)}, bf16[256,128]{1,0:T(8,128)(2,1)S(1)}, u32[]{:S(2)}, u32[]{:S(2)}) collective-permute-start(bf16[256,128]{1,0:T(8,128)(2,1)S(1)} %get-tuple-element.17.own_ref), channel_id=1, source_target_pairs={{0,4},{4,0},{1,5},{5,1},{2,6},{6,2},{3,7},{7,3},{8,12},{12,8},{9,1... | collective-permute-start | bytes 196616 | tf_op jit(solution)/shard_map/ppermute | solution.py:145

commit v8 on v7

--- a/solution.py
+++ b/solution.py
@@ -15,7 +15,7 @@
 CUBIC = 0.044715
 MIB = 1024 * 1024
 DEPTH_FIRST = 10
-PLANE_FIRST = 22
+PLANE_FIRST = 23
 VMEM = pl.BlockSpec(memory_space=pltpu.VMEM)
 HBM = pl.BlockSpec(memory_space=pltpu.HBM)
 SMEM = pl.BlockSpec(memory_space=pltpu.SMEM)

time: 59 us -> 59.2 us (level)
  no operation moved by 1% of the time
where the time goes in v8:
time: 59.2 us; the launch traced here: 58.9 us
  blocking collectives  38.4 us (65%)
  starting transfers between devices  13.4 us (23%)
  Pallas kernels  5.57 us (9%)
  between operations  1.42 us (2%)
    all_to_all x1, blocking collectives, body(): lax.all_to_all(partial, 'z', 0, 0, axis_index_groups=groups, tiled=True)  21.9 us
    all_to_all x1, blocking collectives, body(): lax.all_to_all(gradients, PLANE, 0, 0, axis_index_groups=groups, tiled=True)  16.4 us
    ppermute x2, starting transfers between devices, core_swap(): return lax.ppermute(block, 'c', [(0, 1), (1, 0)])  6.78 us
    ppermute x2, starting transfers between devices, cross_swap(): return lax.ppermute(block, SECTION, pairs + [(j, i) for i, j in pairs])  6.65 us
    pallas_call x1, Pallas kernels, body(): pl.pallas_call(layers_kernel, out_shape=jax.ShapeDtypeStruct((plane, dept...  1.64 us
    pallas_call x1, Pallas kernels, body(): pl.pallas_call(functools.partial(own_kernel, groups=plane), out_shape=(ja...  1.25 us
    pallas_call x1, Pallas kernels, body(): pl.pallas_call(adjacency_kernel, out_shape=(jax.ShapeDtypeStruct((3, node...  1.24 us
  transfers between devices with their start and end apart: 4, of which 0 were waited for; matrix products, arithmetic and copies ran while one was open for 0% of the time, Pallas kernels for 5%

profile of v8, /device:TPU:1, one launch (start us, length us, event | category | flops | bytes accessed | tf_op | source)
XLA Modules:
  0.0 58.9 jit_solution(5379316655947733787)
XLA Ops:
  0.6 0.0 copy-start
  0.6 4.7 %collective-permute-start.1 = (bf16[256,128]{1,0:T(8,128)(2,1)}, bf16[256,128]{1,0:T(8,128)(2,1)S(1)}, u32[]{:S(2)}, u32[]{:S(2)}) collective-permute-start(bf16[256,128]{1,0:T(8,128)(2,1)} %bitcast.2), channel_id=1, source_target_pairs={{4,8},{12,16},{20,24},{28,32},{36,40},{44,48},{52,56},{60,64},{68,... | collective-permute-start | bytes 196616 | tf_op jit(solution)/shard_map/ppermute | solution.py:141
  5.4 4.9 %collective-permute-start = (bf16[256,128]{1,0:T(8,128)(2,1)}, bf16[256,128]{1,0:T(8,128)(2,1)S(1)}, u32[]{:S(2)}, u32[]{:S(2)}) collective-permute-start(bf16[256,128]{1,0:T(8,128)(2,1)} %bitcast.3), channel_id=1, source_target_pairs={{0,4},{4,0},{1,5},{5,1},{2,6},{6,2},{3,7},{7,3},{8,12},{12,8},{9,1... | collective-permute-start | bytes 196616 | tf_op jit(solution)/shard_map/ppermute | solution.py:145
  10.9 1.2 %adjacency.1 = (bf16[3,256,256]{2,1,0:T(8,128)(2,1)S(1)}, f32[256,128]{1,0:T(8,128)S(1)}) custom-call(s32[1]{0:T(128)} %bitcast.odd_ref, s32[1,1]{1,0:T(1,128)S(6)} %copy.10.count_ref, s32[1,8]{1,0:T(1,128)} %rows_hbm.1, s32[1,8]{1,0:T(1,128)} %cols_hbm.1, bf16[1,8,128,128]{3,2,1,0:T(8,128)(2,1)} %tiles_hbm.1, bf16[1,256,128]{2,1,0:T(8,128)(2,1)} %own_hbm.1), custom_call_target="tpu_custom_call" | custom-call | tf_op jit(solution)/shard_map/adjacency/pallas_call | solution.py:159
  12.1 0.0 collective-permute-done.1.cross_ref
  12.1 0.0 collective-permute-done.other_ref
  12.2 0.0 copy-start.1
  12.2 0.2 aggregate.1
  12.4 1.9 %collective-permute-start.2 = (bf16[272,128]{1,0:T(8,128)(2,1)S(1)}, bf16[272,128]{1,0:T(8,128)(2,1)S(1)}, u32[]{:S(2)}, u32[]{:S(2)}) collective-permute-start(bf16[272,128]{1,0:T(8,128)(2,1)S(1)} %get-tuple-element.16), channel_id=1, source_target_pairs={{4,8},{12,16},{20,24},{28,32},{36,40},{44,48},{52,56},{60,64},{68,... | collective-permute-start | bytes 208904 | tf_op jit(solution)/shard_map/ppermute | solution.py:141
  14.3 1.9 %collective-permute-start.3 = (bf16[256,128]{1,0:T(8,128)(2,1)S(1)}, bf16[256,128]{1,0:T(8,128)(2,1)S(1)}, u32[]{:S(2)}, u32[]{:S(2)}) collective-permute-start(bf16[256,128]{1,0:T(8,128)(2,1)S(1)} %get-tuple-element.17.own_ref), channel_id=1, source_target_pairs={{0,4},{4,0},{1,5},{5,1},{2,6},{6,2},{3,7},{7,3},{8,12},{12,8},{9,1... | collective-permute-start | bytes 196616 | tf_op jit(solution)/shard_map/ppermute | solution.py:145
  16.3 0.0 copy-done
  16.3 0.0 copy-done.1
  16.3 1.3 %own_part.1 = (f32[256,512]{1,0:T(8,128)S(1)}, f32[256,512]{1,0:T(8,128)S(1)}, bf16[768,256]{1,0:T(8,128)(2,1)S(1)}, bf16[128,512]{1,0:T(8,128)(2,1)S(1)}, bf16[...) custom-call(bf16[3,256,256]{2,1,0:T(8,128)(2,1)S(1)} %get-tuple-element.14.adj_ref, ...), custom_call_target="tpu_custom_call" | custom-call | flops 600000000 | bytes 4194304 | tf_op jit(solution)/shard_map/own_part/pallas_call | solution.py:187
  17.5 0.0 collective-permute-done.3.other_ref
  17.5 0.6 %other_part.1 = (f32[256,512]{1,0:T(8,128)S(1)}, f32[256,512]{1,0:T(8,128)S(1)}) custom-call(bf16[3,256,256]{2,1,0:T(8,128)(2,1)S(1)} %get-tuple-element.14.adj_ref, bf16[256,128]{1,0:T(8,128)(2,1)S(1)} %collective-permute-done.3.other_ref, bf16[128,512]{1,0:T(8,128)(2,1)S(1)} %get-tuple-element.19.w1_ref, f32[256,512]{1,0:T(8,128)S(1)} %get-tuple-element.20.near_ref), custom_call_target="tpu_custom_call" | custom-call | tf_op jit(solution)/shard_map/other_part/pallas_call | solution.py:204
  18.2 0.0 collective-permute-done.2.cross_ref
  18.2 1.6 %layers.1 = bf16[32,16,640]{2,1,0:T(8,128)(2,1)S(1)} custom-call(bf16[3,256,256]{2,1,0:T(8,128)(2,1)S(1)} %get-tuple-element.14.adj_ref, bf16[272,128]{1,0:T(8,128)(2,1)S(1)} %collective-permute-done.2.cross_ref, bf16[256,128]{1,0:T(8,128)(2,1)S(1)} %get-tuple-element.17.own_ref, bf16[256,128]{1,0:T(8,128)(2,1)S(1)} %collective-permute-done.3.other_ref, ...), custom_call_target="tpu_custom_call" | custom-call | tf_op jit(solution)/shard_map/layers/pallas_call | solution.py:215
  19.8 16.4 %all_to_all.10 = bf16[32,16,640]{2,1,0:T(8,128)(2,1)S(1)} all-to-all(bf16[32,16,640]{2,1,0:T(8,128)(2,1)S(1)} %layers.1), channel_id=1, replica_groups={{23,24,25,26,27,28,29,30,31,0,1,2,3,4,5,6,7,8,9,10,11,12,13,14,15,16,17..., dimensions={0} | all-to-all | bytes 1310720 | tf_op jit(solution)/shard_map/all_to_all | solution.py:225
  36.2 0.1 reduce_sum.12
  36.4 21.9 %all_to_all.11.in_ref = bf16[16,5,128]{2,1,0:T(8,128)(2,1)S(1)} all-to-all(bf16[16,5,128]{2,1,0:T(8,128)(2,1)S(1)} %reshape.11), channel_id=1, replica_groups={{320,352,384,416,448,480,0,32,64,96,128,160,192,224,256,288},{321,353,3..., dimensions={0} | all-to-all | bytes 40960 | tf_op jit(solution)/shard_map/all_to_all | solution.py:229
  58.3 0.6 %depth_sum.1 = (f32[1,128]{1,0:T(1,128)}, f32[1,512]{1,0:T(1,128)}) custom-call(bf16[16,5,128]{2,1,0:T(8,128)(2,1)S(1)} %all_to_all.11.in_ref), custom_call_target="tpu_custom_call" | custom-call | tf_op jit(solution)/shard_map/depth_sum/pallas_call | solution.py:230
  (1 shorter events, 0.0 us)
Async XLA Ops:
  0.6 15.6 %copy-start = (bf16[512,512]{1,0:T(8,128)(2,1)S(1)}, bf16[512,512]{1,0:T(8,128)(2,1)}, u32[]{:S(2)}) copy-start(bf16[512,512]{1,0:T(8,128)(2,1)} %w2_ref.1) | copy-start | bytes 1572868
  0.6 11.5 %collective-permute-start.1 = (bf16[256,128]{1,0:T(8,128)(2,1)}, bf16[256,128]{1,0:T(8,128)(2,1)S(1)}, u32[]{:S(2)}, u32[]{:S(2)}) collective-permute-start(bf16[256,128]{1,0:T(8,128)(2,1)} %bitcast.2), channel_id=1, source_target_pairs={{4,8},{12,16},{20,24},{28,32},{36,40},{44,48},{52,56},{60,64},{68,... | collective-permute-start | bytes 196616 | tf_op jit(solution)/shard_map/ppermute | solution.py:141
  5.4 6.8 %collective-permute-start = (bf16[256,128]{1,0:T(8,128)(2,1)}, bf16[256,128]{1,0:T(8,128)(2,1)S(1)}, u32[]{:S(2)}, u32[]{:S(2)}) collective-permute-start(bf16[256,128]{1,0:T(8,128)(2,1)} %bitcast.3), channel_id=1, source_target_pairs={{0,4},{4,0},{1,5},{5,1},{2,6},{6,2},{3,7},{7,3},{8,12},{12,8},{9,1... | collective-permute-start | bytes 196616 | tf_op jit(solution)/shard_map/ppermute | solution.py:145
  12.2 4.1 %copy-start.1 = (bf16[128,512]{1,0:T(8,128)(2,1)S(1)}, bf16[128,512]{1,0:T(8,128)(2,1)}, u32[]{:S(2)}) copy-start(bf16[128,512]{1,0:T(8,128)(2,1)} %w1_ref.1) | copy-start | bytes 393220
  12.4 5.8 %collective-permute-start.2 = (bf16[272,128]{1,0:T(8,128)(2,1)S(1)}, bf16[272,128]{1,0:T(8,128)(2,1)S(1)}, u32[]{:S(2)}, u32[]{:S(2)}) collective-permute-start(bf16[272,128]{1,0:T(8,128)(2,1)S(1)} %get-tuple-element.16), channel_id=1, source_target_pairs={{4,8},{12,16},{20,24},{28,32},{36,40},{44,48},{52,56},{60,64},{68,... | collective-permute-start | bytes 208904 | tf_op jit(solution)/shard_map/ppermute | solution.py:141
  14.3 3.2 %collective-permute-start.3 = (bf16[256,128]{1,0:T(8,128)(2,1)S(1)}, bf16[256,128]{1,0:T(8,128)(2,1)S(1)}, u32[]{:S(2)}, u32[]{:S(2)}) collective-permute-start(bf16[256,128]{1,0:T(8,128)(2,1)S(1)} %get-tuple-element.17.own_ref), channel_id=1, source_target_pairs={{0,4},{4,0},{1,5},{5,1},{2,6},{6,2},{3,7},{7,3},{8,12},{12,8},{9,1... | collective-permute-start | bytes 196616 | tf_op jit(solution)/shard_map/ppermute | solution.py:145

commit v9 on v7

--- a/solution.py
+++ b/solution.py
@@ -14,7 +14,7 @@
 SCALE = 0.7978845608028654
 CUBIC = 0.044715
 MIB = 1024 * 1024
-DEPTH_FIRST = 10
+DEPTH_FIRST = 11
 PLANE_FIRST = 22
 VMEM = pl.BlockSpec(memory_space=pltpu.VMEM)
 HBM = pl.BlockSpec(memory_space=pltpu.HBM)

time: 59 us -> 59.1 us (level)
  no operation moved by 1% of the time
where the time goes in v9:
time: 59.1 us; the launch traced here: 58.6 us
  blocking collectives  38 us (64%)
  starting transfers between devices  13.4 us (23%)
  Pallas kernels  5.63 us (10%)
  between operations  1.42 us (2%)
    all_to_all x1, blocking collectives, body(): lax.all_to_all(partial, 'z', 0, 0, axis_index_groups=groups, tiled=True)  22 us
    all_to_all x1, blocking collectives, body(): lax.all_to_all(gradients, PLANE, 0, 0, axis_index_groups=groups, tiled=True)  16 us
    ppermute x2, starting transfers between devices, core_swap(): return lax.ppermute(block, 'c', [(0, 1), (1, 0)])  6.78 us
    ppermute x2, starting transfers between devices, cross_swap(): return lax.ppermute(block, SECTION, pairs + [(j, i) for i, j in pairs])  6.65 us
    pallas_call x1, Pallas kernels, body(): pl.pallas_call(layers_kernel, out_shape=jax.ShapeDtypeStruct((plane, dept...  1.64 us
    pallas_call x1, Pallas kernels, body(): pl.pallas_call(adjacency_kernel, out_shape=(jax.ShapeDtypeStruct((3, node...  1.3 us
    pallas_call x1, Pallas kernels, body(): pl.pallas_call(functools.partial(own_kernel, groups=plane), out_shape=(ja...  1.25 us
  transfers between devices with their start and end apart: 4, of which 0 were waited for; matrix products, arithmetic and copies ran while one was open for 0% of the time, Pallas kernels for 5%

profile of v9, /device:TPU:1, one launch (start us, length us, event | category | flops | bytes accessed | tf_op | source)
XLA Modules:
  0.0 58.6 jit_solution(9658504399940432960)
XLA Ops:
  0.6 0.0 copy-start
  0.6 4.7 %collective-permute-start.1 = (bf16[256,128]{1,0:T(8,128)(2,1)}, bf16[256,128]{1,0:T(8,128)(2,1)S(1)}, u32[]{:S(2)}, u32[]{:S(2)}) collective-permute-start(bf16[256,128]{1,0:T(8,128)(2,1)} %bitcast.2), channel_id=1, source_target_pairs={{4,8},{12,16},{20,24},{28,32},{36,40},{44,48},{52,56},{60,64},{68,... | collective-permute-start | bytes 196616 | tf_op jit(solution)/shard_map/ppermute | solution.py:141
  5.4 4.9 %collective-permute-start = (bf16[256,128]{1,0:T(8,128)(2,1)}, bf16[256,128]{1,0:T(8,128)(2,1)S(1)}, u32[]{:S(2)}, u32[]{:S(2)}) collective-permute-start(bf16[256,128]{1,0:T(8,128)(2,1)} %bitcast.3), channel_id=1, source_target_pairs={{0,4},{4,0},{1,5},{5,1},{2,6},{6,2},{3,7},{7,3},{8,12},{12,8},{9,1... | collective-permute-start | bytes 196616 | tf_op jit(solution)/shard_map/ppermute | solution.py:145
  10.9 1.3 %adjacency.1 = (bf16[3,256,256]{2,1,0:T(8,128)(2,1)S(1)}, f32[256,128]{1,0:T(8,128)S(1)}) custom-call(s32[1]{0:T(128)} %bitcast.odd_ref, s32[1,1]{1,0:T(1,128)S(6)} %copy.10.count_ref, s32[1,8]{1,0:T(1,128)} %rows_hbm.1, s32[1,8]{1,0:T(1,128)} %cols_hbm.1, bf16[1,8,128,128]{3,2,1,0:T(8,128)(2,1)} %tiles_hbm.1, bf16[1,256,128]{2,1,0:T(8,128)(2,1)} %own_hbm.1), custom_call_target="tpu_custom_call" | custom-call | tf_op jit(solution)/shard_map/adjacency/pallas_call | solution.py:159
  12.2 0.0 collective-permute-done.1.cross_ref
  12.2 0.0 collective-permute-done.other_ref
  12.2 0.0 copy-start.1
  12.2 0.2 aggregate.1
  12.5 1.9 %collective-permute-start.2 = (bf16[272,128]{1,0:T(8,128)(2,1)S(1)}, bf16[272,128]{1,0:T(8,128)(2,1)S(1)}, u32[]{:S(2)}, u32[]{:S(2)}) collective-permute-start(bf16[272,128]{1,0:T(8,128)(2,1)S(1)} %get-tuple-element.16), channel_id=1, source_target_pairs={{4,8},{12,16},{20,24},{28,32},{36,40},{44,48},{52,56},{60,64},{68,... | collective-permute-start | bytes 208904 | tf_op jit(solution)/shard_map/ppermute | solution.py:141
  14.4 1.9 %collective-permute-start.3 = (bf16[256,128]{1,0:T(8,128)(2,1)S(1)}, bf16[256,128]{1,0:T(8,128)(2,1)S(1)}, u32[]{:S(2)}, u32[]{:S(2)}) collective-permute-start(bf16[256,128]{1,0:T(8,128)(2,1)S(1)} %get-tuple-element.17.own_ref), channel_id=1, source_target_pairs={{0,4},{4,0},{1,5},{5,1},{2,6},{6,2},{3,7},{7,3},{8,12},{12,8},{9,1... | collective-permute-start | bytes 196616 | tf_op jit(solution)/shard_map/ppermute | solution.py:145
  16.3 0.0 copy-done
  16.3 0.0 copy-done.1
  16.3 1.3 %own_part.1 = (f32[256,512]{1,0:T(8,128)S(1)}, f32[256,512]{1,0:T(8,128)S(1)}, bf16[768,256]{1,0:T(8,128)(2,1)S(1)}, bf16[128,512]{1,0:T(8,128)(2,1)S(1)}, bf16[...) custom-call(bf16[3,256,256]{2,1,0:T(8,128)(2,1)S(1)} %get-tuple-element.14.adj_ref, ...), custom_call_target="tpu_custom_call" | custom-call | flops 600000000 | bytes 4194304 | tf_op jit(solution)/shard_map/own_part/pallas_call | solution.py:187
  17.6 0.0 collective-permute-done.3.other_ref
  17.6 0.6 %other_part.1 = (f32[256,512]{1,0:T(8,128)S(1)}, f32[256,512]{1,0:T(8,128)S(1)}) custom-call(bf16[3,256,256]{2,1,0:T(8,128)(2,1)S(1)} %get-tuple-element.14.adj_ref, bf16[256,128]{1,0:T(8,128)(2,1)S(1)} %collective-permute-done.3.other_ref, bf16[128,512]{1,0:T(8,128)(2,1)S(1)} %get-tuple-element.19.w1_ref, f32[256,512]{1,0:T(8,128)S(1)} %get-tuple-element.20.near_ref), custom_call_target="tpu_custom_call" | custom-call | tf_op jit(solution)/shard_map/other_part/pallas_call | solution.py:204
  18.2 0.0 collective-permute-done.2.cross_ref
  18.2 1.6 %layers.1 = bf16[32,16,640]{2,1,0:T(8,128)(2,1)S(1)} custom-call(bf16[3,256,256]{2,1,0:T(8,128)(2,1)S(1)} %get-tuple-element.14.adj_ref, bf16[272,128]{1,0:T(8,128)(2,1)S(1)} %collective-permute-done.2.cross_ref, bf16[256,128]{1,0:T(8,128)(2,1)S(1)} %get-tuple-element.17.own_ref, bf16[256,128]{1,0:T(8,128)(2,1)S(1)} %collective-permute-done.3.other_ref, ...), custom_call_target="tpu_custom_call" | custom-call | tf_op jit(solution)/shard_map/layers/pallas_call | solution.py:215
  19.9 16.0 %all_to_all.10 = bf16[32,16,640]{2,1,0:T(8,128)(2,1)S(1)} all-to-all(bf16[32,16,640]{2,1,0:T(8,128)(2,1)S(1)} %layers.1), channel_id=1, replica_groups={{22,23,24,25,26,27,28,29,30,31,0,1,2,3,4,5,6,7,8,9,10,11,12,13,14,15,16..., dimensions={0} | all-to-all | bytes 1310720 | tf_op jit(solution)/shard_map/all_to_all | solution.py:225
  35.9 0.1 reduce_sum.12
  36.1 22.0 %all_to_all.11.in_ref = bf16[16,5,128]{2,1,0:T(8,128)(2,1)S(1)} all-to-all(bf16[16,5,128]{2,1,0:T(8,128)(2,1)S(1)} %reshape.11), channel_id=1, replica_groups={{352,384,416,448,480,0,32,64,96,128,160,192,224,256,288,320},{353,385,4..., dimensions={0} | all-to-all | bytes 40960 | tf_op jit(solution)/shard_map/all_to_all | solution.py:229
  58.0 0.6 %depth_sum.1 = (f32[1,128]{1,0:T(1,128)}, f32[1,512]{1,0:T(1,128)}) custom-call(bf16[16,5,128]{2,1,0:T(8,128)(2,1)S(1)} %all_to_all.11.in_ref), custom_call_target="tpu_custom_call" | custom-call | tf_op jit(solution)/shard_map/depth_sum/pallas_call | solution.py:230
  (1 shorter events, 0.0 us)
Async XLA Ops:
  0.6 15.7 %copy-start = (bf16[512,512]{1,0:T(8,128)(2,1)S(1)}, bf16[512,512]{1,0:T(8,128)(2,1)}, u32[]{:S(2)}) copy-start(bf16[512,512]{1,0:T(8,128)(2,1)} %w2_ref.1) | copy-start | bytes 1572868
  0.6 11.6 %collective-permute-start.1 = (bf16[256,128]{1,0:T(8,128)(2,1)}, bf16[256,128]{1,0:T(8,128)(2,1)S(1)}, u32[]{:S(2)}, u32[]{:S(2)}) collective-permute-start(bf16[256,128]{1,0:T(8,128)(2,1)} %bitcast.2), channel_id=1, source_target_pairs={{4,8},{12,16},{20,24},{28,32},{36,40},{44,48},{52,56},{60,64},{68,... | collective-permute-start | bytes 196616 | tf_op jit(solution)/shard_map/ppermute | solution.py:141
  5.4 6.8 %collective-permute-start = (bf16[256,128]{1,0:T(8,128)(2,1)}, bf16[256,128]{1,0:T(8,128)(2,1)S(1)}, u32[]{:S(2)}, u32[]{:S(2)}) collective-permute-start(bf16[256,128]{1,0:T(8,128)(2,1)} %bitcast.3), channel_id=1, source_target_pairs={{0,4},{4,0},{1,5},{5,1},{2,6},{6,2},{3,7},{7,3},{8,12},{12,8},{9,1... | collective-permute-start | bytes 196616 | tf_op jit(solution)/shard_map/ppermute | solution.py:145
  12.2 4.1 %copy-start.1 = (bf16[128,512]{1,0:T(8,128)(2,1)S(1)}, bf16[128,512]{1,0:T(8,128)(2,1)}, u32[]{:S(2)}) copy-start(bf16[128,512]{1,0:T(8,128)(2,1)} %w1_ref.1) | copy-start | bytes 393220
  12.5 5.8 %collective-permute-start.2 = (bf16[272,128]{1,0:T(8,128)(2,1)S(1)}, bf16[272,128]{1,0:T(8,128)(2,1)S(1)}, u32[]{:S(2)}, u32[]{:S(2)}) collective-permute-start(bf16[272,128]{1,0:T(8,128)(2,1)S(1)} %get-tuple-element.16), channel_id=1, source_target_pairs={{4,8},{12,16},{20,24},{28,32},{36,40},{44,48},{52,56},{60,64},{68,... | collective-permute-start | bytes 208904 | tf_op jit(solution)/shard_map/ppermute | solution.py:141
  14.4 3.2 %collective-permute-start.3 = (bf16[256,128]{1,0:T(8,128)(2,1)S(1)}, bf16[256,128]{1,0:T(8,128)(2,1)S(1)}, u32[]{:S(2)}, u32[]{:S(2)}) collective-permute-start(bf16[256,128]{1,0:T(8,128)(2,1)S(1)} %get-tuple-element.17.own_ref), channel_id=1, source_target_pairs={{0,4},{4,0},{1,5},{5,1},{2,6},{6,2},{3,7},{7,3},{8,12},{12,8},{9,1... | collective-permute-start | bytes 196616 | tf_op jit(solution)/shard_map/ppermute | solution.py:145
